TPU v7x, 128 devices: a whole 4x4x4 slice. The times are simulated.
128 devices in a mesh: row: 8 (over y, core), col: 16 (over x, z).
Axes of the slice: x: 4, y: 4, z: 4, core: 2. Of those that a mesh axis runs over, the one named last changes fastest.
Arguments:
- kernel: float32 [8, 2048, 4, 4096], P(None, 'row', None, 'col'), may hold values from 0 to 8, as said below
Outputs:
- factored: float32 [8, 2048, 4, 4096], P(None, 'row', None, 'col')
Inputs may be any that keep to these rules, and one draw needn't show every extreme that they name: `kernel`: symmetric positive definite.
All inputs are finite; a program needn't handle non-finite values.
Results may differ from a plain program's by a relative error of at most 0.0003.
Values sent between devices are 32-bit elements; how exact they have to be, the bound alone decides.
A program may use at most 192 MiB of HBM per device.

v0:
```python
import jax
import jax.numpy as jnp
from jax import lax
from jax.sharding import PartitionSpec as P

NB = 1024


def spread(block, axis, source):
    block = jnp.where(lax.axis_index(axis) == source, block, jnp.zeros_like(block))
    return lax.psum(block, axis)


def solve_rows(prepared, rows):
    return lax.linalg.triangular_solve(
        prepared, rows, left_side=False, lower=True, transpose_a=True
    )


def per_device(kernel):
    row_count = kernel.shape[0]
    tile_size = kernel.shape[1]
    col_count = kernel.shape[2]
    panel_width = NB
    panel_tiles = panel_width // tile_size
    local_rows = row_count * tile_size
    local_cols = col_count * tile_size
    n_rows = lax.axis_size("row")
    n_cols = lax.axis_size("col")
    row_index = lax.axis_index("row")
    col_index = lax.axis_index("col")
    matrix = kernel.reshape(local_rows, local_cols)
    own_tile = kernel[0, :, 0, :]
    diag_pieces = []
    for source in range(panel_tiles):
        diag_pieces.append(spread(own_tile, "row", source))
    diag_strip = jnp.concatenate(diag_pieces, axis=0)
    panel_tile = matrix[:, :tile_size]
    panels = []
    strips = []
    for source in range(panel_tiles):
        got_panel, got_strip = (
            spread(panel_tile, "col", source),
            spread(diag_strip, "col", source),
        )
        panels.append(got_panel)
        strips.append(got_strip)
    panel_rows = jnp.concatenate(panels, axis=1)
    leading = jnp.concatenate(strips, axis=1)
    lower_factor = jnp.linalg.cholesky(leading)
    solved = solve_rows(lower_factor, panel_rows)
    first_start = jnp.minimum(row_index, panel_tiles - 1) * tile_size
    factor_rows = lax.dynamic_slice_in_dim(lower_factor, first_start, tile_size, 0)
    first_rows = jnp.where(row_index < panel_tiles, factor_rows, solved[:tile_size])
    lower_rows = jnp.concatenate([first_rows, solved[tile_size:]], axis=0)
    ratio = n_cols // n_rows
    grouped = lower_rows.reshape(col_count, ratio, tile_size, panel_width)
    picked = lax.dynamic_index_in_dim(grouped, col_index // n_rows, axis=1, keepdims=False)
    column_side = spread(picked, "row", col_index % n_rows)
    column_side = column_side.reshape(local_cols, panel_width)
    product = lax.dot_general(
        lower_rows,
        column_side,
        (((1,), (1,)), ((), ())),
        precision=lax.Precision.HIGHEST,
        preferred_element_type=jnp.float32,
    )
    updated = matrix - product
    tile_rows = jnp.arange(row_count, dtype=jnp.int32)[:, None]
    inner = jnp.arange(tile_size, dtype=jnp.int32)[None, :]
    global_rows = ((tile_rows * n_rows + row_index) * tile_size + inner).reshape(local_rows)
    tile_cols = jnp.arange(col_count, dtype=jnp.int32)[:, None]
    global_cols = ((tile_cols * n_cols + col_index) * tile_size + inner).reshape(local_cols)
    trailing = (global_rows >= panel_width)[:, None] & (global_cols >= panel_width)[None, :]
    col_start = jnp.minimum(col_index, panel_tiles - 1) * tile_size
    panel_block = lax.dynamic_slice_in_dim(lower_rows, col_start, tile_size, 1)
    panel_part = jnp.concatenate(
        [panel_block, jnp.zeros((local_rows, local_cols - tile_size), jnp.float32)], axis=1
    )
    in_panel = (global_cols < panel_width)[None, :]
    result = jnp.where(trailing, updated, jnp.where(in_panel, panel_part, 0.0))
    return result.reshape(row_count, tile_size, col_count, tile_size)


def solution(mesh):
    in_specs = (P(None, "row", None, "col"),)
    out_specs = P(None, "row", None, "col")
    return jax.shard_map(
        per_device, mesh=mesh, in_specs=in_specs, out_specs=out_specs, check_vma=False
    )
```

profile of v0, /device:TPU:18, one launch (start us, length us, event | category | flops | bytes accessed | tf_op | source)
XLA Modules:
  0.0 832.2 jit_solution(379024861326014615)
XLA Ops:
  21.6 49.3 %all-reduce.12.cloned.1.call-done = (f32[256,256]{0,1:T(8,128)}, f32[256,256]{0,1:T(8,128)}, f32[256,256]{0,1:T(8,128)}, f32[256,256]{0,1:T(8,128)}) async-done(((f32[256,256]{0,1:T(8,128)}, f32[256,256]{0,1:T(8,128)}, f32[256,256]{0,1:T(8,128)}, f32[256,256]{0,1:T(8,128)}), (f32[256,256]{0,1:T(8,128)}, f32[256,256]{0,1:T(8,128)}, f32[256,256]{0,1:T(8,128)}, ...) | async-done | bytes 1048592 | tf_op jit(solution)/shard_map/psum | solution.py:11
  77.1 184.9 %all-reduce.10.cloned.1.call-done = (f32[2048,256]{1,0:T(8,128)}, f32[1024,256]{0,1:T(8,128)}, f32[1024,256]{0,1:T(8,128)}, f32[1024,256]{0,1:T(8,128)}, f32[102...) async-done(((f32[2048,256]{1,0:T(8,128)}, f32[1024,256]{0,1:T(8,128)}, f32[1024,256]{0,1:T(8,128)}, f32[1024,256]{0,1:T(8,128)}, ...) | async-done | bytes 12582928 | tf_op jit(solution)/shard_map/psum | solution.py:11
  281.3 11.7 %cholesky.223 = f32[128,128]{1,0:T(8,128)S(1)} custom-call(f32[128,128]{1,0:T(8,128)S(1)} %cholesky.580), custom_call_target="Cholesky" | custom-call | tf_op jit(solution)/shard_map/jit(cholesky)/cholesky | solution.py:50
  295.5 9.8 %custom-call.62 = f32[1,128,128]{1,2,0:T(8,128)S(1)} custom-call(f32[1,128,128]{2,1,0:T(8,128)S(1)} %get-tuple-element.87), custom_call_target="InvertDiagBlocksLowerTriangular" | custom-call | tf_op jit(solution)/shard_map/jit(cholesky)/cholesky | solution.py:50
  309.3 11.9 %cholesky.244 = f32[128,128]{1,0:T(8,128)S(1)} custom-call(f32[128,128]{1,0:T(8,128)S(1)} %cholesky.584), custom_call_target="Cholesky" | custom-call | tf_op jit(solution)/shard_map/jit(cholesky)/cholesky | solution.py:50
  321.8 9.8 %custom-call.63 = f32[1,128,128]{1,2,0:T(8,128)S(1)} custom-call(f32[1,128,128]{2,1,0:T(8,128)S(1)} %get-tuple-element.84), custom_call_target="InvertDiagBlocksLowerTriangular" | custom-call | tf_op jit(solution)/shard_map/jit(cholesky)/cholesky | solution.py:50
  334.9 11.7 %cholesky.468 = f32[128,128]{1,0:T(8,128)S(1)} custom-call(f32[128,128]{1,0:T(8,128)S(1)} %cholesky.589), custom_call_target="Cholesky" | custom-call | tf_op jit(solution)/shard_map/jit(cholesky)/cholesky | solution.py:50
  348.0 9.8 %custom-call.64 = f32[1,128,128]{1,2,0:T(8,128)S(1)} custom-call(f32[1,128,128]{2,1,0:T(8,128)S(1)} %get-tuple-element.81), custom_call_target="InvertDiagBlocksLowerTriangular" | custom-call | tf_op jit(solution)/shard_map/jit(cholesky)/cholesky | solution.py:50
  361.3 11.9 %cholesky.487 = f32[128,128]{1,0:T(8,128)S(1)} custom-call(f32[128,128]{1,0:T(8,128)S(1)} %cholesky.594), custom_call_target="Cholesky" | custom-call | tf_op jit(solution)/shard_map/jit(cholesky)/cholesky | solution.py:50
  374.5 9.8 %custom-call.65 = f32[1,128,128]{1,2,0:T(8,128)S(1)} custom-call(f32[1,128,128]{2,1,0:T(8,128)S(1)} %get-tuple-element.78), custom_call_target="InvertDiagBlocksLowerTriangular" | custom-call | tf_op jit(solution)/shard_map/jit(cholesky)/cholesky | solution.py:50
  387.7 11.7 %cholesky.506 = f32[128,128]{1,0:T(8,128)S(1)} custom-call(f32[128,128]{1,0:T(8,128)S(1)} %cholesky.599), custom_call_target="Cholesky" | custom-call | tf_op jit(solution)/shard_map/jit(cholesky)/cholesky | solution.py:50
  400.8 10.2 %custom-call.66 = f32[1,128,128]{1,2,0:T(8,128)S(1)} custom-call(f32[1,128,128]{2,1,0:T(8,128)S(1)} %get-tuple-element.75), custom_call_target="InvertDiagBlocksLowerTriangular" | custom-call | tf_op jit(solution)/shard_map/jit(cholesky)/cholesky | solution.py:50
  414.3 11.7 %cholesky.526 = f32[128,128]{1,0:T(8,128)S(1)} custom-call(f32[128,128]{1,0:T(8,128)S(1)} %cholesky.604), custom_call_target="Cholesky" | custom-call | tf_op jit(solution)/shard_map/jit(cholesky)/cholesky | solution.py:50
  440.1 11.9 %cholesky.546 = f32[128,128]{1,0:T(8,128)S(1)} custom-call(f32[128,128]{1,0:T(8,128)S(1)} %cholesky.609), custom_call_target="Cholesky" | custom-call | tf_op jit(solution)/shard_map/jit(cholesky)/cholesky | solution.py:50
  453.3 9.8 %custom-call.68 = f32[1,128,128]{1,2,0:T(8,128)S(1)} custom-call(f32[1,128,128]{2,1,0:T(8,128)S(1)} %get-tuple-element.69), custom_call_target="InvertDiagBlocksLowerTriangular" | custom-call | tf_op jit(solution)/shard_map/jit(cholesky)/cholesky | solution.py:50
  465.7 11.7 %cholesky.564 = f32[128,128]{1,0:T(8,128)S(1)} custom-call(f32[128,128]{1,0:T(8,128)S(1)} %convolution_subtract_fusion.11), custom_call_target="Cholesky" | custom-call | tf_op jit(solution)/shard_map/jit(cholesky)/cholesky | solution.py:50
  491.4 28.3 %while.1 = (s32[]{:T(128)}, f32[1024,1024]{1,0:T(8,128)}, s32[8,2]{0,1:T(2,128)S(1)}, f32[8,128,128]{2,1,0:T(8,128)}, s32[]{:T(128)}) while((s32[]{:T(128)}, f32[1024,1024]{1,0:T(8,128)}, s32[8,2]{0,1:T(2,128)S(1)}, f32[8,128,128]{2,1,0:T(8,128)}, s32[]{:T(128)}) %tuple.64), condition=%wide.while_cond, body=%wide.while_body.sunk | while | flops 2 | bytes 132705 | solution.py:15
  519.6 80.2 %custom-call.69 = f32[8,128,128]{1,2,0:T(8,128)} custom-call(f32[8,128,128]{2,1,0:T(8,128)} %get-tuple-element.12), custom_call_target="InvertDiagBlocksLowerTriangular" | custom-call | tf_op jit(solution)/shard_map/triangular_solve | solution.py:15
  649.4 10.9 %convolution_subtract_fusion.2 = f32[2048,128]{1,0:T(8,128)S(1)} fusion(f32[2048,640]{0,1:T(8,128)} %get-tuple-element.45, f32[2048,256]{1,0:T(8,128)S(1)} %copy-done.14, f32[1024,1024]{1,0:T(8,128)} %get-tuple-element.173), kind=kOutput, calls=%fused_computation.30 | convolution fusion | flops 2013528064 | bytes 7667712 | tf_op jit(solution)/shard_map/triangular_solve | solution.py:15
  664.1 12.1 %convolution_subtract_fusion = f32[2048,128]{1,0:T(8,128)S(1)} fusion(f32[2048,768]{0,1:T(8,128)} %get-tuple-element.42, f32[2048,256]{1,0:T(8,128)S(1)} %copy-done.3, f32[1024,1024]{1,0:T(8,128)} %get-tuple-element.173), kind=kOutput, calls=%fused_computation.27 | convolution fusion | flops 2416181248 | bytes 8781824 | tf_op jit(solution)/shard_map/triangular_solve | solution.py:15
  679.1 14.2 %convolution_subtract_fusion.1 = f32[2048,128]{1,0:T(8,128)S(1)} fusion(f32[2048,896]{0,1:T(8,128)} %get-tuple-element.98, f32[2048,256]{1,0:T(8,128)S(1)} %copy-done.3, f32[1024,1024]{1,0:T(8,128)} %get-tuple-element.173), kind=kOutput, calls=%fused_computation.29 | convolution fusion | flops 2818834432 | bytes 9895936 | tf_op jit(solution)/shard_map/triangular_solve | solution.py:15
  714.5 66.2 %all-reduce.8.cloned.1.call-done = f32[1024,1024]{1,0:T(8,128)} async-done(((f32[1024,1024]{1,0:T(8,128)}), f32[1024,1024]{1,0:T(8,128)}) %all-reduce.8.cloned.1.call-update) | async-done | bytes 4194320 | tf_op jit(solution)/shard_map/psum | solution.py:11
  780.7 34.2 %select_select_fusion = f32[2048,1024]{1,0:T(8,128)} fusion(f32[2048,256]{1,0:T(8,128)S(1)} %fusion.22, f32[2048,1024]{1,0:T(8,128)} %bitcast.118, pred[1024]{0:T(1024)(128)(4,1)S(1)} %lt.34, pred[1024]{0:T(1024)(128)(4,1)S(1)} %ge.33, pred[2048]{0:T(1024)(128)(4,1)S(1)} %ge.31, f32[1024,1024]{1,0:T(8,128)} %all-reduce.8.cloned.1.call-done, ...), kind=kOutput, calls=%fused_computation.5 | convolution fusion | flops 25780289536 | bytes 31461376 | tf_op jit(solution)/shard_map/dot_general | solution.py:61
  814.9 10.5 %reshape.156 = f32[8,256,4,256]{3,2,1,0:T(4,128)} reshape(f32[2048,1024]{1,0:T(8,128)} %select_select_fusion) | data formatting | bytes 16777216 | tf_op jit(solution)/shard_map/reshape | solution.py:82
  (156 shorter events, 197.4 us)
Async XLA Ops:
  6.5 64.4 %all-reduce.12.cloned.1.call-start = ((), (), s32[]{:S(2)}) async-start(), calls=%async_computation.2 | async-start | bytes 2097152 | tf_op jit(solution)/shard_map/psum | solution.py:11
  9.1 252.9 %all-reduce.10.cloned.1.call-start = ((), (), s32[]{:S(2)}) async-start(), calls=%async_computation.1 | async-start | bytes 25165824 | tf_op jit(solution)/shard_map/psum | solution.py:11
  14.7 3.4 copy-start.1
  77.0 703.7 %all-reduce.8.cloned.1.call-start = ((), (), s32[]{:S(2)}) async-start(), calls=%async_computation | async-start | bytes 8388608 | tf_op jit(solution)/shard_map/psum | solution.py:11
  262.0 4.9 copy-start.13
  262.0 6.0 copy-start.12
  279.3 1.9 copy-start.2
  484.5 115.4 %copy-start.10 = (f32[2048,256]{1,0:T(8,128)S(1)}, f32[2048,256]{1,0:T(8,128)}, u32[]{:S(2)}) copy-start(f32[2048,256]{1,0:T(8,128)} %get-tuple-element.21) | copy-start | bytes 6291460
  603.6 6.6 copy-start.11
  645.2 4.2 copy-start.14
  649.4 14.7 %copy-start.3 = (f32[2048,256]{1,0:T(8,128)S(1)}, f32[2048,256]{1,0:T(8,128)}, u32[]{:S(2)}) copy-start(f32[2048,256]{1,0:T(8,128)} %get-tuple-element.28) | copy-start | bytes 6291460
  693.4 8.0 copy-start.5
  694.7 6.9 copy-start.4
  699.9 1.9 copy-start.6
  699.9 2.0 copy-start.9
  701.4 1.3 copy-start.8
  701.6 1.4 copy-start.7
  706.4 3.8 copy-start
Sparse Core Ops, SparseCore 0:
  9.9 60.9 all-reduce.11
  77.1 184.8 all-reduce.9
  712.7 67.9 all-reduce.7
where the time goes:
time: 843 us; the launch traced here: 832 us
  waiting for transfers between devices  300 us (36%)
  other arithmetic  279 us (33%)
  matrix products  146 us (17%)
  local copies, waits for them, and re-layouts  88.1 us (10%)
  between operations  18.9 us (2%)
    psum x3, waiting for transfers between devices, spread(): return lax.psum(block, axis)  300 us
    another operation x30, other arithmetic, per_device(): lower_factor = jnp.linalg.cholesky(leading)  172 us
    another operation x15, matrix products, solve_rows(): lax.linalg.triangular_solve(prepared, rows, left_side=False, lower=True,...  88.7 us
    another operation x3, other arithmetic, solve_rows(): lax.linalg.triangular_solve(prepared, rows, left_side=False, lower=True,...  87.1 us
    dot_general x1, matrix products, per_device(): lax.dot_general(lower_rows, column_side, (((1,), (1,)), ((), ())), precis...  34.2 us
    another operation x24, local copies, waits for them, and re-layouts  28.3 us
    another operation x14, matrix products, per_device(): lower_factor = jnp.linalg.cholesky(leading)  23.1 us
    unnamed x45, local copies, waits for them, and re-layouts  23 us
  transfers between devices with their start and end apart: 3, of which 3 were waited for; matrix products, arithmetic and copies ran while one was open for 1% of the time, Pallas kernels for 0%

commit v1 on v0

v1 whole, which is shorter than its diff:
```python
import functools

import jax
import jax.numpy as jnp
from jax import lax
from jax.experimental import pallas as pl
from jax.experimental.pallas import tpu as pltpu
from jax.sharding import PartitionSpec as P

F32=jnp.float32; BF=jnp.bfloat16

def split(a):
    hi=a.astype(BF)
    return hi,(a-hi.astype(F32)).astype(BF)
NN=(((1,),(0,)),((),())); NT=(((1,),(1,)),((),())); TN=(((0,),(0,)),((),()))
def dot3(a,b,dims=NN):
    d=functools.partial(lax.dot_general,dimension_numbers=dims,preferred_element_type=F32)
    return d(a[0],b[0])+(d(a[0],b[1])+d(a[1],b[0]))

def finish_kernel(pos,ker,rows,cols,u_ref,w_ref,out,uh,ul,wh,wl,yh,yl,xh,xl,xp):
    t=pl.program_id(0); r=pos[0]; c=pos[1]
    T=256
    @pl.when(t==0)
    def _():
        for k in range(4):
            uh[k*T:(k+1)*T,:],ul[k*T:(k+1)*T,:]=split(u_ref[k*T:(k+1)*T,:])
            wh[k],wl[k]=split(w_ref[k])
        for k in range(4):
            acc=cols[k*T:(k+1)*T,:]
            for j in range(k):
                acc=acc-dot3((uh[j*T:(j+1)*T,k*T:(k+1)*T],ul[j*T:(j+1)*T,k*T:(k+1)*T]),(yh[j*T:(j+1)*T,:],yl[j*T:(j+1)*T,:]),TN)
            y=dot3((wh[k],wl[k]),split(acc))
            yh[k*T:(k+1)*T,:],yl[k*T:(k+1)*T,:]=split(y)
    lead=jnp.logical_and(t==0,r<4)
    @pl.when(lead)
    def _():
        out[...]=jnp.zeros_like(out)
        @pl.when(c<4)
        def _():
            blk=u_ref[pl.ds(pl.multiple_of(jnp.minimum(c,3)*T,T),T),pl.ds(pl.multiple_of(jnp.minimum(r,3)*T,T),T)]
            out[0,:,0,:]=blk.T
    @pl.when(jnp.logical_not(lead))
    def _():
        for k in range(4):
            ks=slice(k*T,(k+1)*T)
            acc=rows[:,ks]
            for j in range(k):
                js=slice(j*T,(j+1)*T)
                acc=acc-dot3((xh[:,js],xl[:,js]),(uh[js,ks],ul[js,ks]))
            x=dot3(split(acc),(wh[k],wl[k]),NT)
            xh[:,ks],xl[:,ks]=split(x)
            xp[:,ks]=x
        for uu in range(4):
            us=slice(uu*T,(uu+1)*T)
            s=dot3((xh[...],xl[...]),(yh[:,us],yl[:,us]))
            out[0,:,uu,:]=ker[0,:,uu,:]-s
        @pl.when(c<4)
        def _():
            out[0,:,0,:]=xp[:,pl.ds(pl.multiple_of(jnp.minimum(c,3)*T,T),T)]

def finish(pos,kernel,rows,cols,u,w):
    full=lambda shape: pl.BlockSpec(shape,lambda t:(0,)*len(shape),pipeline_mode=pl.Buffered(1))
    return pl.pallas_call(finish_kernel,grid=(8,),
        in_specs=[pl.BlockSpec(memory_space=pltpu.SMEM),pl.BlockSpec((1,256,4,256),lambda t:(t,0,0,0)),
                  pl.BlockSpec((256,1024),lambda t:(t,0)),full((1024,1024)),full((1024,1024)),full((4,256,256))],
        out_specs=pl.BlockSpec((1,256,4,256),lambda t:(t,0,0,0)),
        out_shape=jax.ShapeDtypeStruct((8,256,4,256),F32),
        scratch_shapes=[pltpu.VMEM((1024,1024),BF)]*2+[pltpu.VMEM((4,256,256),BF)]*2+[pltpu.VMEM((1024,1024),BF)]*2+[pltpu.VMEM((256,1024),BF)]*2+[pltpu.VMEM((256,1024),F32)],
        compiler_params=pltpu.CompilerParams(vmem_limit_bytes=56<<20),name="finish")(pos,kernel,rows,cols,u,w)

HI=lax.Precision.HIGHEST
def bc(x,i,n=8): return jnp.broadcast_to(x[i:i+1,:],(n,x.shape[1]))
def dotx(a,b,dims=NN): return lax.dot_general(a,b,dims,precision=HI,preferred_element_type=F32)
def leaf(V, c0, b, u_ref, w_ref, r0, mb):
    nt=b//8; mt=mb//8
    VT=[[V[8*t:8*t+8,128*h:128*h+128] for h in range(2)] for t in range(nt)]
    refs=[u_ref,w_ref]
    for s in range(0,nt,mt):
        C=[[jnp.broadcast_to(VT[t][0][:, c0+8*s+j:c0+8*s+j+1],(8,128)) if t>=s+j//8 else None for t in range(nt)] for j in range(mb)]
        d=bc(C[0][s],0)
        for k in range(mb):
            tk=s+k//8
            ck=C[k]
            q=pltpu.reciprocal(d,approx=False)
            rs=lax.rsqrt(d)
            if k+1<mb:
                sb=bc(ck[s+(k+1)//8],(k+1)%8)
                p=bc(C[k+1][s+(k+1)//8],(k+1)%8)
                d=p-(sb*sb)*q
            m=[ck[t]*q if t>=tk else None for t in range(nt)]
            v=[bc(VT[tk][h],k%8) for h in range(2)]
            for h in range(2): refs[h][r0+8*s+k:r0+8*s+k+1,:]=(v[h]*rs)[:1]
            for j in range(k+1,mb):
                cj=bc(ck[s+j//8],j%8)
                for t in range(s+j//8,nt):
                    C[j][t]=C[j][t]-m[t]*cj
            for t in range(s+(k+1)//8,nt):
                for h in range(2):
                    VT[t][h]=VT[t][h]-m[t]*v[h]
def iotas(n,m):
    return lax.broadcasted_iota(jnp.int32,(n,m),0),lax.broadcasted_iota(jnp.int32,(n,m),1)
def block128(D,us,ws,b=32,mb=16):
    ii,jj=iotas(128,128)
    I=(ii==jj).astype(F32)
    for s in range(128//b):
        r0=s*b
        V=jnp.concatenate([D[r0:r0+b],I[r0:r0+b]],axis=1)
        if s:
            up=us[:r0,:]; wp=ws[:r0,:]
            V=V-dotx(up[:,r0:r0+b], jnp.concatenate([up,wp],axis=1),TN)
        leaf(V,r0,b,us,ws,r0,mb)

def chol_loop(u,w,us,ws):
    B=128
    def step(k,_):
        ko=pl.multiple_of(k*B,B)
        block128(u[pl.ds(ko,B),pl.ds(ko,B)],us,ws)
        ii,jj=iotas(B,B)
        W=jnp.where(jj<=ii,ws[...],0.0)
        ws[...]=W
        ri,ci=iotas(B,1024)
        U=jnp.where(ci>=ri+ko,dotx(W,u[pl.ds(ko,B),:]),0.0)
        u[pl.ds(ko,B),:]=U
        def upd(j,_):
            jo=pl.multiple_of(j*B,B)
            u[pl.ds(jo,B),:]=u[pl.ds(jo,B),:]-dotx(u[pl.ds(ko,B),pl.ds(jo,B)],U_ref[...] if False else u[pl.ds(ko,B),:],TN)
            return 0
        lax.fori_loop(k+1,8,upd,0)
        h=k//2
        @pl.when(k%2==0)
        def _():
            w[pl.ds(h,1),:B,:B]=W[None]
            w[pl.ds(h,1),:B,B:]=jnp.zeros((1,B,B),F32)
        @pl.when(k%2==1)
        def _():
            W1=w[pl.ds(h,1),:B,:B][0]
            kp=pl.multiple_of(ko-B,B)
            L21=dotx(u[pl.ds(kp,B),pl.ds(ko,B)],W1,TN)
            w[pl.ds(h,1),B:,B:]=W[None]
            w[pl.ds(h,1),B:,:B]=-dotx(W,L21)[None]
        return 0
    lax.fori_loop(0,8,step,0)
def chol_kernel(a_ref,u,w,us,ws):
    u[...]=a_ref[...]
    chol_loop(u,w,us,ws)
def chol(a):
    return pl.pallas_call(chol_kernel,out_shape=[jax.ShapeDtypeStruct((1024,1024),F32),jax.ShapeDtypeStruct((4,256,256),F32)],
        in_specs=[pl.BlockSpec(memory_space=pltpu.VMEM)],out_specs=[pl.BlockSpec(memory_space=pltpu.VMEM)]*2,
        scratch_shapes=[pltpu.VMEM((128,128),F32)]*2,compiler_params=pltpu.CompilerParams(vmem_limit_bytes=48<<20),name="factor")(a)

def from_first_four(x, pieces):
    n=x.shape[0]//4
    xs=x.reshape(4,n,x.shape[1])
    c=lax.axis_index("col")
    got=xs[0]
    for d in (1,2,3):
        g=lax.ppermute(xs[d],"col",[(z,4*d+z) for z in range(4)])
        got=jnp.where(c//4==d,g,got)
    allp=lax.all_gather(got,"col",axis=0)
    return allp.reshape(4,4,n,x.shape[1]).transpose(1,0,2,3).reshape(4,4*n,x.shape[1])


def per_device(kernel):
    r=lax.axis_index("row"); c=lax.axis_index("col")
    pcol=kernel[:,:,0,:].reshape(2048,256)
    strip=kernel[0].transpose(1,0,2)
    half=strip.reshape(4,2,128,256)
    g=lax.ppermute(half[:,1],"row",[(i,i+4) for i in range(4)])
    piece=jnp.where(r<4,half[:,0],g)
    gat=lax.all_gather(piece,"row",axis=0)
    cols=gat.reshape(2,4,4,128,256).transpose(1,0,3,2,4).reshape(1024,1024)
    lead=from_first_four(cols[:,:256],4).transpose(1,0,2).reshape(1024,1024)
    rows=from_first_four(pcol,4).transpose(1,0,2).reshape(2048,1024)
    u,w=chol(lead)
    pos=jnp.stack([r,c]).astype(jnp.int32)
    return finish(pos,kernel,rows,cols,u,w)


def solution(mesh):
    spec=P(None,"row",None,"col")
    return jax.shard_map(per_device,mesh=mesh,in_specs=(spec,),out_specs=spec,check_vma=False)
```

time: 843 us -> 283 us (0.34); the launches traced: 832 us -> 282 us
  other arithmetic: 279 us -> 4.17 us
  waiting for transfers between devices: 300 us -> 122 us
  matrix products: 146 us -> 0 us
  Pallas kernels: 0 us -> 91.9 us
  local copies, waits for them, and re-layouts: 88.1 us -> 43.8 us
    psum x3 -> x0, waiting for transfers between devices: 300 us -> none  [spread(): return lax.psum(block, axis)]
    another operation x33 -> x1, other arithmetic: 260 us -> 0.65 us  [per_device(): pos = jnp.stack([r, c]).astype(jnp.int32)]
    another operation x29 -> x0, matrix products: 112 us -> none  [the longest x15 88.7 us: solve_rows(): lax.linalg.triangular_solve(prepared, rows, left_side=False, lower=True,...]
    pallas_call x0 -> x2, Pallas kernels: none -> 91.9 us  [the longest x1 50.9 us: chol(): pl.pallas_call(chol_kernel, out_shape=[jax.ShapeDtypeStruct((1024, 1024),...]
    ppermute x0 -> x7, waiting for transfers between devices: none -> 62.3 us  [the longest x6 46.5 us: from_first_four(): g = lax.ppermute(xs[d], 'col', [(z, 4 * d + z) for z in range(4)])]
    all_gather x0 -> x3, waiting for transfers between devices: none -> 59.7 us  [the longest x1 33.1 us: per_device(): gat = lax.all_gather(piece, 'row', axis=0)]
    another operation x40 -> x0, local copies, waits for them, and re-layouts: 43.8 us -> none
    dot_general x1 -> x0, matrix products: 34.2 us -> none  [per_device(): lax.dot_general(lower_rows, column_side, (((1,), (1,)), ((), ())), precis...]
  transfers between devices with their start and end apart: 3 -> 10, of which waited for: 3 -> 6; matrix products, arithmetic and copies ran while one was open for 1% -> 4% of each run, Pallas kernels for 0% -> 18%
where the time goes in v1:
time: 283 us; the launch traced here: 282 us
  waiting for transfers between devices  122 us (43%)
  Pallas kernels  91.9 us (32%)
  local copies, waits for them, and re-layouts  43.8 us (15%)
  between operations  13.3 us (5%)
  starting transfers between devices  6.7 us (2%)
  other arithmetic  4.17 us (1%)
    pallas_call x1, Pallas kernels, chol(): pl.pallas_call(chol_kernel, out_shape=[jax.ShapeDtypeStruct((1024, 1024),...  50.9 us
    ppermute x6, waiting for transfers between devices, from_first_four(): g = lax.ppermute(xs[d], 'col', [(z, 4 * d + z) for z in range(4)])  46.5 us
    pallas_call x1, Pallas kernels, finish(): pl.pallas_call(finish_kernel, grid=(8,), in_specs=[pl.BlockSpec(memory_sp...  41 us
    all_gather x1, waiting for transfers between devices, per_device(): gat = lax.all_gather(piece, 'row', axis=0)  33.1 us
    all_gather x2, waiting for transfers between devices, from_first_four(): allp = lax.all_gather(got, 'col', axis=0)  26.6 us
    ppermute x1, waiting for transfers between devices, per_device(): g = lax.ppermute(half[:, 1], 'row', [(i, i + 4) for i in range(4)])  15.8 us
    unnamed x13, local copies, waits for them, and re-layouts  14.9 us
    transpose x1, local copies, waits for them, and re-layouts, from_first_four(): allp.reshape(4, 4, n, x.shape[1]).transpose(1, 0, 2, 3)  12.2 us
  transfers between devices with their start and end apart: 10, of which 6 were waited for; matrix products, arithmetic and copies ran while one was open for 4% of the time, Pallas kernels for 18%

profile of v1, /device:TPU:18, one launch (start us, length us, event | category | flops | bytes accessed | tf_op | source)
XLA Modules:
  0.0 282.0 jit_solution(13774954019965914280)
XLA Ops:
  6.5 1.4 slice.55
  8.2 1.3 collective-permute-start.3
  9.5 15.8 %collective-permute-done.3 = f32[4,128,256]{2,1,0:T(8,128)S(1)} collective-permute-done((f32[4,128,256]{2,1,0:T(8,128)S(1)}, f32[4,128,256]{2,1,0:T(8,128)S(1)}, u32[]{:S(2)}, u32[]{:S(2)}) %collective-permute-start.3) | collective-permute-done | bytes 524320 | tf_op jit(solution)/shard_map/ppermute | solution.py:168
  26.2 33.1 %all-gather.9.cloned.1.call-done = f32[32,128,256]{2,1,0:T(8,128)} async-done(((f32[4,128,256]{2,1,0:T(8,128)}), f32[32,128,256]{2,1,0:T(8,128)}) %all-gather.9.cloned.1.call-update) | async-done | bytes 4194320 | tf_op jit(solution)/shard_map/all_gather | solution.py:170
  59.3 4.9 %copy.28 = f32[4,2,128,4,256]{4,3,2,1,0:T(4,128)S(1)} copy(f32[4,2,128,4,256]{4,2,3,0,1:T(8,128)} %bitcast.56) | data formatting | bytes 8388608 | tf_op jit(solution)/shard_map/transpose | solution.py:171
  64.2 1.0 copy.39
  65.2 2.0 copy-done.2
  67.2 1.3 collective-permute-start.6
  69.9 8.3 %collective-permute-done.6 = f32[256,256]{1,0:T(8,128)S(1)} collective-permute-done((f32[256,256]{1,0:T(8,128)S(1)}, f32[256,256]{1,0:T(8,128)S(1)}, u32[]{:S(2)}, u32[]{:S(2)}) %collective-permute-start.6) | collective-permute-done | bytes 262176 | tf_op jit(solution)/shard_map/ppermute | solution.py:157
  78.3 1.7 fusion.4
  80.1 5.0 %fusion.5 = (f32[2,256,1,256]{3,2,1,0:T(1,128)S(1)}, f32[2,256,1,256]{3,2,1,0:T(1,128)S(1)}, f32[2,256,1,256]{3,2,1,0:T(1,128)S(1)}, f32[2,256,1,256]{3,2,1,0:T(1,128)S(1)}) fusion(f32[8,256,4,256]{3,2,1,0:T(4,128)} %ker.1), kind=kLoop, calls=%fused_computation.10 | loop fusion | bytes 4194304 | tf_op jit(solution)/shard_map/slice | solution.py:155
  86.6 1.3 collective-permute-start.2
  88.0 38.2 %collective-permute-done.2 = f32[512,256]{1,0:T(8,128)S(1)} collective-permute-done((f32[512,256]{1,0:T(8,128)S(1)}, f32[512,256]{1,0:T(8,128)S(1)}, u32[]{:S(2)}, u32[]{:S(2)}) %collective-permute-start.2) | collective-permute-done | bytes 524320 | tf_op jit(solution)/shard_map/ppermute | solution.py:157
  126.2 0.9 fusion.2
  127.8 13.0 %all-gather.11.cloned.1.call-done = f32[4096,256]{1,0:T(8,128)} async-done(((f32[256,256]{1,0:T(8,128)}), f32[4096,256]{1,0:T(8,128)}) %all-gather.11.cloned.1.call-update) | async-done | bytes 4194320 | tf_op jit(solution)/shard_map/all_gather | solution.py:159
  140.8 2.6 copy.29
  143.5 2.7 copy.37
  146.1 50.9 %factor.1 = (f32[1024,1024]{1,0:T(8,128)S(1)}, f32[4,256,256]{2,1,0:T(8,128)S(1)}) custom-call(f32[1024,1024]{1,0:T(8,128)} %bitcast.51), custom_call_target="tpu_custom_call" | custom-call | tf_op jit(solution)/shard_map/factor/pallas_call | solution.py:147
  197.0 1.9 copy-done
  198.9 1.0 copy-done.1
  199.9 13.6 %all-gather.7.cloned.1.call-done = f32[8192,256]{1,0:T(8,128)} async-done(((f32[512,256]{1,0:T(8,128)}), f32[8192,256]{1,0:T(8,128)}) %all-gather.7.cloned.1.call-update) | async-done | bytes 8388624 | tf_op jit(solution)/shard_map/all_gather | solution.py:159
  213.5 12.2 %copy.25 = f32[4,4,512,256]{3,0,2,1:T(4,128)} copy(f32[4,4,512,256]{3,2,0,1:T(8,128)} %bitcast.54) | data formatting | bytes 16777216 | tf_op jit(solution)/shard_map/transpose | solution.py:160
  225.7 8.7 %copy.38 = f32[256,8,4,256]{3,1,2,0:T(8,128)} copy(f32[256,8,4,256]{3,2,1,0:T(4,128)} %bitcast.47) | data formatting | bytes 16777216
  234.4 41.0 %finish.1 = f32[8,256,4,256]{3,2,1,0:T(4,128)} custom-call(s32[2]{0:T(128)} %pad_add_fusion.pos, f32[8,256,4,256]{3,2,1,0:T(4,128)} %ker.1, f32[2048,1024]{1,0:T(8,128)} %bitcast.46, f32[1024,1024]{1,0:T(8,128)} %bitcast.50, f32[1024,1024]{1,0:T(8,128)} %copy-done, f32[4,256,256]{2,1,0:T(8,128)} %copy-done.1), custom_call_target="tpu_custom_call" | custom-call | tf_op jit(solution)/shard_map/finish/pallas_call | solution.py:63
  (26 shorter events, 4.9 us)
Async XLA Ops:
  6.5 52.7 %all-gather.9.cloned.1.call-start = ((), (), s32[]{:S(2)}) async-start(), calls=%async_computation.1 | async-start | bytes 4718592 | tf_op jit(solution)/shard_map/all_gather | solution.py:170
  8.2 17.1 %collective-permute-start.3 = (f32[4,128,256]{2,1,0:T(8,128)S(1)}, f32[4,128,256]{2,1,0:T(8,128)S(1)}, u32[]{:S(2)}, u32[]{:S(2)}) collective-permute-start(f32[4,128,256]{2,1,0:T(8,128)S(1)} %slice_bitcast_fusion), channel_id=1, source_target_pairs={{0,64},{16,80},{32,96},{48,112},{1,65},{17,81},{33,97},{49,113},{2... | collective-permute-start | bytes 1572872 | tf_op jit(solution)/shard_map/ppermute | solution.py:168
  26.1 114.7 %all-gather.11.cloned.1.call-start = ((), (), s32[]{:S(2)}) async-start(), calls=%async_computation.2 | async-start | bytes 4456448 | tf_op jit(solution)/shard_map/all_gather | solution.py:159
  65.2 2.0 copy-start.2
  67.2 11.0 %collective-permute-start.6 = (f32[256,256]{1,0:T(8,128)S(1)}, f32[256,256]{1,0:T(8,128)S(1)}, u32[]{:S(2)}, u32[]{:S(2)}) collective-permute-start(f32[256,256]{1,0:T(8,128)S(1)} %get-tuple-element.13), channel_id=1, source_target_pairs={{0,4},{1,5},{2,6},{3,7},{16,20},{17,21},{18,22},{19,23},{32,36},{3... | collective-permute-start | bytes 786440 | tf_op jit(solution)/shard_map/ppermute | solution.py:157
  68.5 9.7 %collective-permute-start.5 = (f32[256,256]{1,0:T(8,128)S(1)}, f32[256,256]{1,0:T(8,128)S(1)}, u32[]{:S(2)}, u32[]{:S(2)}) collective-permute-start(f32[256,256]{1,0:T(8,128)S(1)} %get-tuple-element.14), channel_id=1, source_target_pairs={{0,8},{1,9},{2,10},{3,11},{16,24},{17,25},{18,26},{19,27},{32,40},... | collective-permute-start | bytes 786440 | tf_op jit(solution)/shard_map/ppermute | solution.py:157
  69.2 9.1 %collective-permute-start.4 = (f32[256,256]{1,0:T(8,128)S(1)}, f32[256,256]{1,0:T(8,128)S(1)}, u32[]{:S(2)}, u32[]{:S(2)}) collective-permute-start(f32[256,256]{1,0:T(8,128)S(1)} %get-tuple-element.15), channel_id=1, source_target_pairs={{0,12},{1,13},{2,14},{3,15},{16,28},{17,29},{18,30},{19,31},{32,44... | collective-permute-start | bytes 786440 | tf_op jit(solution)/shard_map/ppermute | solution.py:157
  80.0 133.5 %all-gather.7.cloned.1.call-start = ((), (), s32[]{:S(2)}) async-start(), calls=%async_computation | async-start | bytes 8912896 | tf_op jit(solution)/shard_map/all_gather | solution.py:159
  85.1 2.8 %collective-permute-start = (f32[512,256]{1,0:T(8,128)S(1)}, f32[512,256]{1,0:T(8,128)S(1)}, u32[]{:S(2)}, u32[]{:S(2)}) collective-permute-start(f32[512,256]{1,0:T(8,128)S(1)} %bitcast.59), channel_id=1, source_target_pairs={{0,12},{1,13},{2,14},{3,15},{16,28},{17,29},{18,30},{19,31},{32,44... | collective-permute-start | bytes 1572872 | tf_op jit(solution)/shard_map/ppermute | solution.py:157
  85.9 2.1 collective-permute-start.1
  86.6 39.6 %collective-permute-start.2 = (f32[512,256]{1,0:T(8,128)S(1)}, f32[512,256]{1,0:T(8,128)S(1)}, u32[]{:S(2)}, u32[]{:S(2)}) collective-permute-start(f32[512,256]{1,0:T(8,128)S(1)} %bitcast.61), channel_id=1, source_target_pairs={{0,4},{1,5},{2,6},{3,7},{16,20},{17,21},{18,22},{19,23},{32,36},{3... | collective-permute-start | bytes 1572872 | tf_op jit(solution)/shard_map/ppermute | solution.py:157
  197.0 1.9 copy-start
  198.9 1.0 copy-start.1
Sparse Core Ops, SparseCore 0:
  26.3 32.9 all-gather.8
  80.1 60.6 all-gather.10
  143.0 70.5 all-gather.6

commit v2 on v1

--- a/solution.py
+++ b/solution.py
@@ -26,7 +26,7 @@
             uh[k*T:(k+1)*T,:],ul[k*T:(k+1)*T,:]=split(u_ref[k*T:(k+1)*T,:])
             wh[k],wl[k]=split(w_ref[k])
         for k in range(4):
-            acc=cols[k*T:(k+1)*T,:]
+            acc=jnp.concatenate([cols[k,uu] for uu in range(4)],axis=1)
             for j in range(k):
                 acc=acc-dot3((uh[j*T:(j+1)*T,k*T:(k+1)*T],ul[j*T:(j+1)*T,k*T:(k+1)*T]),(yh[j*T:(j+1)*T,:],yl[j*T:(j+1)*T,:]),TN)
             y=dot3((wh[k],wl[k]),split(acc))
@@ -43,7 +43,7 @@
     def _():
         for k in range(4):
             ks=slice(k*T,(k+1)*T)
-            acc=rows[:,ks]
+            acc=rows[k]
             for j in range(k):
                 js=slice(j*T,(j+1)*T)
                 acc=acc-dot3((xh[:,js],xl[:,js]),(uh[js,ks],ul[js,ks]))
@@ -62,7 +62,7 @@
     full=lambda shape: pl.BlockSpec(shape,lambda t:(0,)*len(shape),pipeline_mode=pl.Buffered(1))
     return pl.pallas_call(finish_kernel,grid=(8,),
         in_specs=[pl.BlockSpec(memory_space=pltpu.SMEM),pl.BlockSpec((1,256,4,256),lambda t:(t,0,0,0)),
-                  pl.BlockSpec((256,1024),lambda t:(t,0)),full((1024,1024)),full((1024,1024)),full((4,256,256))],
+                  pl.BlockSpec((4,256,256),lambda t:(0,t,0)),full((4,4,256,256)),full((1024,1024)),full((4,256,256))],
         out_specs=pl.BlockSpec((1,256,4,256),lambda t:(t,0,0,0)),
         out_shape=jax.ShapeDtypeStruct((8,256,4,256),F32),
         scratch_shapes=[pltpu.VMEM((1024,1024),BF)]*2+[pltpu.VMEM((4,256,256),BF)]*2+[pltpu.VMEM((1024,1024),BF)]*2+[pltpu.VMEM((256,1024),BF)]*2+[pltpu.VMEM((256,1024),F32)],
@@ -110,68 +110,262 @@
             V=V-dotx(up[:,r0:r0+b], jnp.concatenate([up,wp],axis=1),TN)
         leaf(V,r0,b,us,ws,r0,mb)
 
-def chol_loop(u,w,us,ws):
-    B=128
-    def step(k,_):
-        ko=pl.multiple_of(k*B,B)
-        block128(u[pl.ds(ko,B),pl.ds(ko,B)],us,ws)
-        ii,jj=iotas(B,B)
-        W=jnp.where(jj<=ii,ws[...],0.0)
-        ws[...]=W
-        ri,ci=iotas(B,1024)
-        U=jnp.where(ci>=ri+ko,dotx(W,u[pl.ds(ko,B),:]),0.0)
-        u[pl.ds(ko,B),:]=U
-        def upd(j,_):
-            jo=pl.multiple_of(j*B,B)
-            u[pl.ds(jo,B),:]=u[pl.ds(jo,B),:]-dotx(u[pl.ds(ko,B),pl.ds(jo,B)],U_ref[...] if False else u[pl.ds(ko,B),:],TN)
-            return 0
-        lax.fori_loop(k+1,8,upd,0)
-        h=k//2
-        @pl.when(k%2==0)
-        def _():
-            w[pl.ds(h,1),:B,:B]=W[None]
-            w[pl.ds(h,1),:B,B:]=jnp.zeros((1,B,B),F32)
-        @pl.when(k%2==1)
-        def _():
-            W1=w[pl.ds(h,1),:B,:B][0]
-            kp=pl.multiple_of(ko-B,B)
-            L21=dotx(u[pl.ds(kp,B),pl.ds(ko,B)],W1,TN)
-            w[pl.ds(h,1),B:,B:]=W[None]
-            w[pl.ds(h,1),B:,:B]=-dotx(W,L21)[None]
-        return 0
-    lax.fori_loop(0,8,step,0)
-def chol_kernel(a_ref,u,w,us,ws):
-    u[...]=a_ref[...]
-    chol_loop(u,w,us,ws)
-def chol(a):
-    return pl.pallas_call(chol_kernel,out_shape=[jax.ShapeDtypeStruct((1024,1024),F32),jax.ShapeDtypeStruct((4,256,256),F32)],
-        in_specs=[pl.BlockSpec(memory_space=pltpu.VMEM)],out_specs=[pl.BlockSpec(memory_space=pltpu.VMEM)]*2,
-        scratch_shapes=[pltpu.VMEM((128,128),F32)]*2,compiler_params=pltpu.CompilerParams(vmem_limit_bytes=48<<20),name="factor")(a)
-
-def from_first_four(x, pieces):
-    n=x.shape[0]//4
-    xs=x.reshape(4,n,x.shape[1])
-    c=lax.axis_index("col")
-    got=xs[0]
-    for d in (1,2,3):
-        g=lax.ppermute(xs[d],"col",[(z,4*d+z) for z in range(4)])
-        got=jnp.where(c//4==d,g,got)
-    allp=lax.all_gather(got,"col",axis=0)
-    return allp.reshape(4,4,n,x.shape[1]).transpose(1,0,2,3).reshape(4,4*n,x.shape[1])
+
+T=256
+
+
+def flip(dim, x, z):
+    if dim==0: return x+1-2*lax.rem(x,2),z
+    if dim==1: return x,z+1-2*lax.rem(z,2)
+    if dim==2: return 3-x,z
+    return x,3-z
+
+
+def orbit(dims, x, z):
+    out=[(x,z)]
+    for d in dims:
+        out=out+[flip(d,a,b) for a,b in out]
+    return out
+
+
+class Traffic:
+    def __init__(self, send_sems, recv_sems):
+        self.send_sems=send_sems; self.recv_sems=recv_sems
+        self.sent=[]; self.keys={}; self.next=0
+
+    def slots(self, key, n):
+        if key not in self.keys:
+            self.keys[key]=self.next
+            self.next+=n
+        return self.keys[key]
+
+    def send(self, cond, src, dst, sem, row, col):
+        d=pltpu.make_async_remote_copy(src_ref=src,dst_ref=dst,send_sem=self.send_sems.at[len(self.sent)],recv_sem=self.recv_sems.at[sem],
+            device_id={"row":row,"col":col},device_id_type=pl.DeviceIdType.MESH)
+        if cond is None: d.start()
+        else: pl.when(cond)(lambda: d.start())
+        self.sent.append((cond,d))
+        return len(self.sent)-1
+
+    def settle(self, n, cond):
+        c,d=self.sent[n]
+        pl.when(both(c,cond))(lambda: d.wait_send())
+
+    def local(self, cond, src, dst):
+        d=pltpu.make_async_copy(src,dst,self.send_sems.at[len(self.sent)])
+        if cond is None: d.start()
+        else: pl.when(cond)(lambda: d.start())
+        self.sent.append((None,None))
+        def wait():
+            if cond is None: d.wait()
+            else: pl.when(cond)(lambda: d.wait())
+        return wait
+
+    def recv(self, cond, dst, sem):
+        d=pltpu.make_async_copy(dst,dst,self.recv_sems.at[sem])
+        if cond is None: d.wait()
+        else: pl.when(cond)(lambda: d.wait())
+
+    def drain(self, settled):
+        for n,(cond,d) in enumerate(self.sent):
+            if d is None or n in settled: continue
+            if cond is None: d.wait_send()
+            else: pl.when(cond)(lambda d=d: d.wait_send())
+
+
+def both(a,b):
+    return b if a is None else jnp.logical_and(a,b)
+
+
+def gather_factor_kernel(panel,strip,row_out,col_out,u,w,us,ws,stage,send_sems,recv_sems):
+    r=lax.axis_index("row"); c=lax.axis_index("col")
+    y=r//2; core=lax.rem(r,2); x=c//4; z=lax.rem(c,4)
+    up=lambda v,n=1: lax.rem(v+n,4)
+    at=lambda yy,kk,xx,zz: (2*yy+kk,4*xx+zz)
+    tr=Traffic(send_sems,recv_sems)
+    bar=pltpu.get_barrier_semaphore()
+    friends=[at(up(y,i),core,x,z) for i in (1,3)]+[at(y,1-core,x,z)]+[at(y,core,up(x,i),z) for i in (1,3)]+[at(y,core,x,up(z,i)) for i in (1,3)]
+    for a,b in friends:
+        pl.semaphore_signal(bar,inc=1,device_id={"row":a,"col":b},device_id_type=pl.DeviceIdType.MESH)
+    pl.semaphore_wait(bar,len(friends))
+
+    tile=lambda k,U: u.at[pl.ds(pl.multiple_of(k*T,T),T),pl.ds(pl.multiple_of(U*T,T),T)]
+    rs=jnp.minimum(r,3)
+    B=tr.slots("B",8); BD=tr.slots("BD",8)
+    low=y<2
+    own=[]
+    def b_first(q):
+        own.append(tr.local(low,strip.at[q],col_out.at[rs,q]))
+        for i in (1,3):
+            a,b=at(up(y,i),core,x,z)
+            tr.send(low,strip.at[q],col_out.at[rs,q],B+jnp.minimum(y,1)*4+q,a,b)
+    b_first(0)
+    x0=x==0; x13=lax.rem(x,2)==1; x2=x==2
+    rowpart=lambda xx,zz,o,n: row_out.at[zz,pl.ds(pl.multiple_of(xx*512+o,128),n),:]
+    CS=tr.slots("CS",1); CST=tr.slots("CST",1); CSF=tr.slots("CSF",2)
+    for xx,h in ((1,0),(3,1)):
+        a,b=at(y,core,xx,z)
+        tr.send(x0,panel.at[1024+256*h:1280+256*h,:],stage,CST,a,b)
+    for xx in (1,3):
+        a,b=at(y,core,xx,z)
+        tr.send(x0,panel.at[512*xx:512*xx+512,:],rowpart(xx,z,0,512),CS,a,b)
+    crow=tr.local(x0,panel.at[0:512,:],rowpart(0,z,0,512))
+    for q in (1,2,3): b_first(q)
+
+    def b_forward(q):
+        f=jnp.clip(3-y,0,1)
+        tr.recv(y>=2,col_out.at[2*f+core,q],B+f*4+q)
+        a,b=at(jnp.clip(5-y,0,3),core,x,z)
+        tr.send(y>=2,col_out.at[2*f+core,q],col_out.at[2*f+core,q],B+f*4+q,a,b)
+    def b_last(q):
+        o=jnp.where(y>=2,y-2,1-y)
+        tr.recv(None,col_out.at[2*o+core,q],B+o*4+q)
+        own[q]()
+    def b_share(q):
+        a,b=at(y,1-core,x,z)
+        for j in (0,1):
+            tr.send(None,col_out.at[2*j+core,q],col_out.at[2*j+core,q],BD+j*4+q,a,b)
+    def b_done(q):
+        for j in (0,1):
+            tr.recv(None,col_out.at[2*j+1-core,q],BD+j*4+q)
+    b_forward(0); b_last(0)
+
+    AX=tr.slots("AX",2); AZ=tr.slots("AZ",4); AF=tr.slots("AF",2); AD=tr.slots("AD",8)
+    kk=lambda j: 2*j+core
+    need=lambda j,U: U>=kk(j)
+    lead_own=[]; lead_sent=[[],[]]
+    for j in (0,1):
+        ok=jnp.logical_and(x0,need(j,z))
+        for xx in (1,3):
+            a,b=at(y,core,xx,z)
+            tr.send(ok,col_out.at[kk(j),0],tile(kk(j),z),AX+j,a,b)
+        lead_own.append(tr.local(ok,col_out.at[kk(j),0],tile(kk(j),z)))
+    for j,xx in ((0,1),(1,3)):
+        ok=jnp.logical_and(x==xx,need(j,z))
+        tr.recv(ok,tile(kk(j),z),AX+j)
+        a,b=at(y,core,2,z)
+        lead_sent[j].append(tr.send(ok,tile(kk(j),z),tile(kk(j),z),AX+j,a,b))
+    for j,xx in ((0,1),(1,3)):
+        lead_own[j]()
+        tr.recv(jnp.logical_and(jnp.logical_and(x!=0,x!=xx),need(j,z)),tile(kk(j),z),AX+j)
+    for j in (0,1):
+        ok=need(j,z)
+        for e,i in ((0,1),(1,3)):
+            a,b=at(y,core,x,up(z,i))
+            lead_sent[j].append(tr.send(ok,tile(kk(j),z),tile(kk(j),z),AZ+2*e+j,a,b))
+        a,b=at(y,1-core,x,z)
+        lead_sent[j].append(tr.send(ok,tile(kk(j),z),tile(kk(j),z),AD+j*4,a,b))
+    tr.recv(x13,stage,CST)
+    a,b=at(y,core,2,z)
+    h=jnp.where(x==3,1,0)
+    tr.send(x13,stage,row_out.at[z,pl.ds(pl.multiple_of(1024+256*h,256),256),:],CSF+h,a,b)
+    for e,i in ((0,3),(1,1)):
+        U=up(z,i)
+        for j in (0,1):
+            ok=need(j,U)
+            tr.recv(ok,tile(kk(j),U),AZ+2*e+j)
+            if e==j:
+                a,b=at(y,core,x,up(z,1 if e==0 else 3))
+                lead_sent[j].append(tr.send(ok,tile(kk(j),U),tile(kk(j),U),AF+j,a,b))
+            a,b=at(y,1-core,x,z)
+            lead_sent[j].append(tr.send(ok,tile(kk(j),U),tile(kk(j),U),AD+j*4+i,a,b))
+    for j in (0,1):
+        U=up(z,2); ok=need(j,U)
+        tr.recv(ok,tile(kk(j),U),AF+j)
+        a,b=at(y,1-core,x,z)
+        lead_sent[j].append(tr.send(ok,tile(kk(j),U),tile(kk(j),U),AD+j*4+2,a,b))
+    AG=tr.slots("AG",60)
+    orders=[[(q+i)%4 for i in range(4)] for q in range(4)]
+    def ag_send(i):
+        for q in range(4):
+            dims=orders[q]
+            xx,zz=flip(dims[i],x,z)
+            a,b=at(y,core,xx,zz)
+            for m,(bx,bz) in enumerate(orbit(dims[:i],x,z)):
+                ref=rowpart(bx,bz,128*q,128)
+                tr.send(None,ref,ref,AG+q*15+(1<<i)-1+m,a,b)
+    def ag_recv(i):
+        for q in range(4):
+            dims=orders[q]
+            xx,zz=flip(dims[i],x,z)
+            for m,(bx,bz) in enumerate(orbit(dims[:i],xx,zz)):
+                tr.recv(None,rowpart(bx,bz,128*q,128),AG+q*15+(1<<i)-1+m)
+    tr.recv(x13,rowpart(x,z,0,512),CS)
+    for e in (0,1):
+        tr.recv(x2,rowpart(x,z,256*e,256),CSF+e)
+    crow()
+    ag_send(0)
+    settled=set()
+    def lead_wait(k):
+        mine=core==k%2
+        for n in lead_sent[k//2]:
+            tr.settle(n,mine)
+            settled.add(n)
+        for i in range(4):
+            U=up(z,i)
+            tr.recv(jnp.logical_and(jnp.logical_not(mine),U>=k),tile(k,U),AD+(k//2)*4+i)
+    def more(n):
+        if n==0:
+            ag_recv(0); ag_send(1)
+            for q in (1,2,3): b_forward(q)
+        elif n==1:
+            ag_recv(1); ag_send(2)
+            for q in (0,1,2,3):
+                if q: b_last(q)
+                b_share(q)
+        elif n==2:
+            ag_recv(2); ag_send(3)
+        elif n==7:
+            ag_recv(3)
+            for q in range(4): b_done(q)
+    chol_events(u,w,us,ws,lead_wait,more)
+    tr.drain(settled)
+
+
+def chol_events(u,w,us,ws,lead_wait,more):
+    H=128
+    for K in range(4):
+        ko=T*K
+        lead_wait(K)
+        if K:
+            u[ko:ko+T,ko:]=u[ko:ko+T,ko:]-dotx(u[:ko,ko:ko+T],u[:ko,ko:],TN)
+            u[ko:ko+T,:ko]=jnp.zeros((T,ko),F32)
+        Ws=[]
+        for h in range(2):
+            o=ko+H*h
+            block128(u[o:o+H,o:o+H],us,ws)
+            ii,jj=iotas(H,H)
+            W=jnp.where(jj<=ii,ws[...],0.0)
+            n=1024-ko
+            ri,ci=iotas(H,n)
+            U=jnp.where(ci>=ri+H*h,dotx(W,u[o:o+H,ko:]),0.0)
+            u[o:o+H,ko:]=U
+            if h==0:
+                u[o+H:o+T,ko:]=u[o+H:o+T,ko:]-dotx(U[:,H:T],U,TN)
+                w[K,:H,:H]=W
+                w[K,:H,H:]=jnp.zeros((H,H),F32)
+                L21=dotx(U[:,H:T],W,TN)
+            else:
+                w[K,H:,H:]=W
+                w[K,H:,:H]=-dotx(W,L21)
+            more(2*K+h)
+
+
+def gather_factor(panel,strip):
+    any_=pl.BlockSpec(memory_space=pl.ANY); vm=pl.BlockSpec(memory_space=pltpu.VMEM)
+    return pl.pallas_call(gather_factor_kernel,
+        out_shape=[jax.ShapeDtypeStruct((4,2048,256),F32),jax.ShapeDtypeStruct((4,4,256,256),F32),
+                   jax.ShapeDtypeStruct((1024,1024),F32),jax.ShapeDtypeStruct((4,256,256),F32)],
+        in_specs=[any_,any_],out_specs=[any_,any_,vm,vm],
+        scratch_shapes=[pltpu.VMEM((128,128),F32)]*2+[pltpu.VMEM((256,256),F32),pltpu.SemaphoreType.DMA((160,)),pltpu.SemaphoreType.DMA((112,))],
+        compiler_params=pltpu.CompilerParams(vmem_limit_bytes=48<<20,collective_id=0,has_side_effects=True),name="gather_factor")(panel,strip)
 
 
 def per_device(kernel):
     r=lax.axis_index("row"); c=lax.axis_index("col")
-    pcol=kernel[:,:,0,:].reshape(2048,256)
+    panel=kernel[:,:,0,:].reshape(2048,256)
     strip=kernel[0].transpose(1,0,2)
-    half=strip.reshape(4,2,128,256)
-    g=lax.ppermute(half[:,1],"row",[(i,i+4) for i in range(4)])
-    piece=jnp.where(r<4,half[:,0],g)
-    gat=lax.all_gather(piece,"row",axis=0)
-    cols=gat.reshape(2,4,4,128,256).transpose(1,0,3,2,4).reshape(1024,1024)
-    lead=from_first_four(cols[:,:256],4).transpose(1,0,2).reshape(1024,1024)
-    rows=from_first_four(pcol,4).transpose(1,0,2).reshape(2048,1024)
-    u,w=chol(lead)
+    rows,cols,u,w=gather_factor(panel,strip)
     pos=jnp.stack([r,c]).astype(jnp.int32)
     return finish(pos,kernel,rows,cols,u,w)
 

time: 283 us -> 163 us (0.58)
  waiting for transfers between devices: 122 us -> 0 us
  Pallas kernels: 91.9 us -> 160 us
  local copies, waits for them, and re-layouts: 43.8 us -> 3 us
  between operations: 13.3 us -> 0.03 us
  starting transfers between devices: 6.7 us -> 0 us
  other arithmetic: 4.17 us -> 0.65 us
    pallas_call x1, Pallas kernels: 50.9 us -> 118 us  [gather_factor(): pl.pallas_call(gather_factor_kernel, out_shape=[jax.ShapeDtypeStruct((4,...]
    ppermute x7 -> x0, waiting for transfers between devices: 62.3 us -> none  [the longest x6 46.5 us: from_first_four(): g = lax.ppermute(xs[d], 'col', [(z, 4 * d + z) for z in range(4)])]
    all_gather x3 -> x0, waiting for transfers between devices: 59.7 us -> none  [the longest x1 33.1 us: per_device(): gat = lax.all_gather(piece, 'row', axis=0)]
    transpose x2 -> x0, local copies, waits for them, and re-layouts: 17.1 us -> none  [the longest x1 12.2 us: from_first_four(): allp.reshape(4, 4, n, x.shape[1]).transpose(1, 0, 2, 3)]
    unnamed x13 -> x4, local copies, waits for them, and re-layouts: 14.9 us -> 1.31 us
    ppermute x7 -> x0, starting transfers between devices: 6.62 us -> none  [the longest x6 5.33 us: from_first_four(): g = lax.ppermute(xs[d], 'col', [(z, 4 * d + z) for z in range(4)])]
    reshape x2 -> x0, local copies, waits for them, and re-layouts: 5.29 us -> none  [the longest x1 2.66 us: per_device(): from_first_four(cols[:, :256], 4).transpose(1, 0, 2).reshape(1024, 1024)]
    slice x2, local copies, waits for them, and re-layouts: 5.08 us -> 0.14 us  [per_device(): panel = kernel[:, :, 0, :].reshape(2048, 256)]
  transfers between devices with their start and end apart: 10 -> 0, of which waited for: 6 -> 0; matrix products, arithmetic and copies ran while one was open for 4% -> 0% of each run, Pallas kernels for 18% -> 0%
where the time goes in v2:
time: 163 us
  Pallas kernels  160 us (98%)
  local copies, waits for them, and re-layouts  3 us (2%)
    pallas_call x1, Pallas kernels, gather_factor(): pl.pallas_call(gather_factor_kernel, out_shape=[jax.ShapeDtypeStruct((4,...  118 us
    pallas_call x1, Pallas kernels, finish(): pl.pallas_call(finish_kernel, grid=(8,), in_specs=[pl.BlockSpec(memory_sp...  41.1 us

profile of v2, /device:TPU:18, one launch (start us, length us, event | category | flops | bytes accessed | tf_op | source)
XLA Modules:
  0.0 163.2 jit_solution(16690758161724895533)
XLA Ops:
  0.0 0.7 pad_add_fusion.pos
  0.7 0.0 slice-start
  0.7 1.6 slice.7
  2.2 0.2 copy.8
  2.4 0.1 slice-done
  2.6 0.1 copy.5
  2.7 118.4 %gather_factor.1 = (f32[4,2048,256]{2,1,0:T(8,128)}, f32[4,4,256,256]{3,2,1,0:T(8,128)}, f32[1024,1024]{1,0:T(8,128)}, f32[4,256,256]{2,1,0:T(8,128)S(1)}) custom-call(f32[2048,256]{1,0:T(8,128)S(1)} %bitcast.8, f32[4,256,256]{2,1,0:T(8,128)S(1)} %bitcast.9), custom_call_target="tpu_custom_call" | custom-call | tf_op jit(solution)/shard_map/gather_factor/pallas_call | solution.py:356
  121.1 0.0 copy-start
  121.2 1.0 copy-done
  122.1 41.1 %finish.1 = f32[8,256,4,256]{3,2,1,0:T(4,128)} custom-call(s32[2]{0:T(128)} %pad_add_fusion.pos, f32[8,256,4,256]{3,2,1,0:T(4,128)} %ker.1, f32[4,2048,256]{2,1,0:T(8,128)} %get-tuple-element.9.rows, f32[4,4,256,256]{3,2,1,0:T(8,128)} %get-tuple-element.10.cols, f32[1024,1024]{1,0:T(8,128)} %get-tuple-element.11.u_ref, f32[4,256,256]{2,1,0:T(8,128)} %copy-done), custom_call_target="tpu_custom_call" | custom-call | tf_op jit(solution)/shard_map/finish/pallas_call | solution.py:63
Async XLA Ops:
  0.7 1.9 %slice-start = ((f32[8,256,4,256]{3,2,1,0:T(4,128)}), f32[8,256,1,256]{3,2,1,0:T(1,128)S(1)}, s32[]{:S(2)}) async-start(f32[8,256,4,256]{3,2,1,0:T(4,128)} %ker.1), calls=%async_computation | async-start | bytes 4194304 | tf_op jit(solution)/shard_map/slice | solution.py:366
  121.1 1.0 copy-start

commit v3 on v2

v3 whole, which is shorter than its diff:
```python
import functools

import jax
import jax.numpy as jnp
from jax import lax
from jax.experimental import pallas as pl
from jax.experimental.pallas import tpu as pltpu
from jax.sharding import PartitionSpec as P

F32=jnp.float32; BF=jnp.bfloat16; T=256

def split(a):
    hi=a.astype(BF)
    return hi,(a-hi.astype(F32)).astype(BF)
NN=(((1,),(0,)),((),())); NT=(((1,),(1,)),((),())); TN=(((0,),(0,)),((),()))
def dot3(a,b,dims=NN):
    d=functools.partial(lax.dot_general,dimension_numbers=dims,preferred_element_type=F32)
    return d(a[0],b[0])+(d(a[0],b[1])+d(a[1],b[0]))

def finish_kernel(pos,ker,rows,l_blk,uh,ul,wh,wl,yh,yl,out,xh,xl,xp):
    t=pl.program_id(0); r=pos[0]; c=pos[1]
    lead=jnp.logical_and(t==0,r<4)
    @pl.when(lead)
    def _():
        out[...]=jnp.zeros_like(out)
        @pl.when(c<4)
        def _():
            out[0,:,0,:]=l_blk[...]
    @pl.when(jnp.logical_not(lead))
    def _():
        for k in range(4):
            ks=slice(k*T,(k+1)*T)
            acc=rows[k]
            if k:
                acc=acc-dot3((xh[:,:k*T],xl[:,:k*T]),(uh[:k*T,ks],ul[:k*T,ks]))
            x=dot3(split(acc),(wh[k],wl[k]),NT)
            xh[:,ks],xl[:,ks]=split(x)
            xp[:,ks]=x
        for uu in range(4):
            us=slice(uu*T,(uu+1)*T)
            s=dot3((xh[...],xl[...]),(yh[:,us],yl[:,us]))
            out[0,:,uu,:]=ker[0,:,uu,:]-s
        @pl.when(c<4)
        def _():
            out[0,:,0,:]=xp[:,pl.ds(pl.multiple_of(jnp.minimum(c,3)*T,T),T)]


def finish(pos,kernel,rows,*rest):
    full=lambda a: pl.BlockSpec(a.shape,lambda t:(0,)*a.ndim,pipeline_mode=pl.Buffered(1))
    return pl.pallas_call(finish_kernel,grid=(8,),
        in_specs=[pl.BlockSpec(memory_space=pltpu.SMEM),pl.BlockSpec((1,256,4,256),lambda t:(t,0,0,0)),
                  pl.BlockSpec((4,256,256),lambda t:(0,t,0))]+[full(a) for a in rest],
        out_specs=pl.BlockSpec((1,256,4,256),lambda t:(t,0,0,0)),
        out_shape=jax.ShapeDtypeStruct((8,256,4,256),F32),
        scratch_shapes=[pltpu.VMEM((256,1024),BF)]*2+[pltpu.VMEM((256,1024),F32)],
        compiler_params=pltpu.CompilerParams(vmem_limit_bytes=56<<20),name="finish")(pos,kernel,rows,*rest)


HI=lax.Precision.HIGHEST
def bc(x,i,n=8): return jnp.broadcast_to(x[i:i+1,:],(n,x.shape[1]))
def dotx(a,b,dims=NN): return lax.dot_general(a,b,dims,precision=HI,preferred_element_type=F32)
def leaf(V, c0, b, u_ref, w_ref, r0, mb):
    nt=b//8; mt=mb//8
    VT=[[V[8*t:8*t+8,128*h:128*h+128] for h in range(2)] for t in range(nt)]
    refs=[u_ref,w_ref]
    for s in range(0,nt,mt):
        C=[[jnp.broadcast_to(VT[t][0][:, c0+8*s+j:c0+8*s+j+1],(8,128)) if t>=s+j//8 else None for t in range(nt)] for j in range(mb)]
        d=bc(C[0][s],0)
        for k in range(mb):
            tk=s+k//8
            ck=C[k]
            q=pltpu.reciprocal(d,approx=False)
            rs=lax.rsqrt(d)
            if k+1<mb:
                sb=bc(ck[s+(k+1)//8],(k+1)%8)
                p=bc(C[k+1][s+(k+1)//8],(k+1)%8)
                d=p-(sb*sb)*q
            m=[ck[t]*q if t>=tk else None for t in range(nt)]
            v=[bc(VT[tk][h],k%8) for h in range(2)]
            for h in range(2): refs[h][r0+8*s+k:r0+8*s+k+1,:]=(v[h]*rs)[:1]
            for j in range(k+1,mb):
                cj=bc(ck[s+j//8],j%8)
                for t in range(s+j//8,nt):
                    C[j][t]=C[j][t]-m[t]*cj
            for t in range(s+(k+1)//8,nt):
                for h in range(2):
                    VT[t][h]=VT[t][h]-m[t]*v[h]
def iotas(n,m):
    return lax.broadcasted_iota(jnp.int32,(n,m),0),lax.broadcasted_iota(jnp.int32,(n,m),1)
def block128(D,us,ws,b=32,mb=16):
    ii,jj=iotas(128,128)
    I=(ii==jj).astype(F32)
    for s in range(128//b):
        r0=s*b
        V=jnp.concatenate([D[r0:r0+b],I[r0:r0+b]],axis=1)
        if s:
            up=us[:r0,:]; wp=ws[:r0,:]
            V=V-dotx(up[:,r0:r0+b], jnp.concatenate([up,wp],axis=1),TN)
        leaf(V,r0,b,us,ws,r0,mb)


def flip(dim, x, z):
    if dim==0: return x+1-2*lax.rem(x,2),z
    if dim==1: return x,z+1-2*lax.rem(z,2)
    if dim==2: return 3-x,z
    return x,3-z


def orbit(dims, x, z):
    out=[(x,z)]
    for d in dims:
        out=out+[flip(d,a,b) for a,b in out]
    return out


class Traffic:
    def __init__(self, send_sems, recv_sems):
        self.send_sems=send_sems; self.recv_sems=recv_sems
        self.sent=[]; self.keys={}; self.next=0

    def slots(self, key, n):
        if key not in self.keys:
            self.keys[key]=self.next
            self.next+=n
        return self.keys[key]

    def send(self, cond, src, dst, sem, row, col):
        d=pltpu.make_async_remote_copy(src_ref=src,dst_ref=dst,send_sem=self.send_sems.at[len(self.sent)],recv_sem=self.recv_sems.at[sem],
            device_id={"row":row,"col":col},device_id_type=pl.DeviceIdType.MESH)
        if cond is None: d.start()
        else: pl.when(cond)(lambda: d.start())
        self.sent.append((cond,d))
        return len(self.sent)-1

    def settle(self, n, cond):
        c,d=self.sent[n]
        c=both(c,cond)
        if c is None: d.wait_send()
        else: pl.when(c)(lambda: d.wait_send())

    def local(self, cond, src, dst):
        d=pltpu.make_async_copy(src,dst,self.send_sems.at[len(self.sent)])
        if cond is None: d.start()
        else: pl.when(cond)(lambda: d.start())
        self.sent.append((None,None))
        def wait():
            if cond is None: d.wait()
            else: pl.when(cond)(lambda: d.wait())
        return wait

    def recv(self, cond, dst, sem):
        d=pltpu.make_async_copy(dst,dst,self.recv_sems.at[sem])
        if cond is None: d.wait()
        else: pl.when(cond)(lambda: d.wait())

    def drain(self, settled):
        for n,(cond,d) in enumerate(self.sent):
            if d is None or n in settled: continue
            if cond is None: d.wait_send()
            else: pl.when(cond)(lambda d=d: d.wait_send())


def both(a,b):
    return b if a is None else a if b is None else jnp.logical_and(a,b)


def gather_factor_kernel(panel,strip,row_out,l_out,uh,ul,wh,wl,yh,yl,u,w,col_out,us,ws,stage,send_sems,recv_sems):
    r=lax.axis_index("row"); c=lax.axis_index("col")
    y=r//2; core=lax.rem(r,2); x=c//4; z=lax.rem(c,4)
    up=lambda v,n=1: lax.rem(v+n,4)
    at=lambda yy,kk,xx,zz: (2*yy+kk,4*xx+zz)
    tr=Traffic(send_sems,recv_sems)
    bar=pltpu.get_barrier_semaphore()
    friends=[at(up(y,i),core,x,z) for i in (1,2,3)]+[at(y,1-core,x,z)]+[at(y,core,up(x,i),z) for i in (1,2,3)]+[at(y,core,x,up(z,i)) for i in (1,2,3)]
    for a,b in friends:
        pl.semaphore_signal(bar,inc=1,device_id={"row":a,"col":b},device_id_type=pl.DeviceIdType.MESH)
    pl.semaphore_wait(bar,len(friends))

    tile=lambda k,U,o=0,n=T: u.at[pl.ds(pl.multiple_of(k*T+o,n),n),pl.ds(pl.multiple_of(U*T,T),T)]
    rs=jnp.minimum(r,3)
    low=y<2
    x0=x==0; x13=lax.rem(x,2)==1; x2=x==2
    rowpart=lambda xx,zz,o,n: row_out.at[zz,pl.ds(pl.multiple_of(xx*512+o,128),n),:]
    kk=lambda j: 2*j+core
    parts=[[(0,0,256)],[(1,0,256),(2,0,256),(3,0,256)]]
    lead_sent=[[] for _ in range(4)]
    def pieces(g):
        for k,o,n in parts[g]:
            key=k*2+(1 if o else 0)
            yield k,o,n,core==k%2,"%d"%key
    def window(k,o,n,q):
        return u.at[pl.ds(pl.multiple_of(k*T+o+n//4*q,n//4),n//4),k*T:]
    def patch(k,o,n,q,U):
        return u.at[pl.ds(pl.multiple_of(k*T+o+n//4*q,n//4),n//4),pl.ds(pl.multiple_of(U*T,T),T)]
    own_lead=[[] for _ in parts]
    def lead_a(g):
        for k,o,n,ok,key in pieces(g):
            sem=tr.slots("LA"+key,1); m=n//4
            go=jnp.logical_and(jnp.logical_and(ok,x0),jnp.logical_and(y==k//2,z>=k))
            src=lambda q: strip.at[0,pl.ds(pl.multiple_of(o+m*q,m),m),:]
            for i in (1,2,3):
                a,b=at(up(y,i),core,x,z)
                tr.send(go,src(up(y,i)),patch(k,o,n,up(y,i),z),sem,a,b)
            own_lead[g].append(tr.local(go,src(y),patch(k,o,n,y,z)))
    def lead_b(g):
        for wait in own_lead[g]: wait()
        for k,o,n,ok,key in pieces(g):
            ref=patch(k,o,n,y,z)
            go=jnp.logical_and(ok,jnp.logical_and(x0,z>=k))
            tr.recv(jnp.logical_and(go,y!=k//2),ref,tr.slots("LA"+key,1))
            sem=tr.slots("LB"+key,1)
            for i in (1,2,3):
                a,b=at(y,core,i,z)
                lead_sent[k].append(tr.send(go,ref,ref,sem,a,b))
    def lead_c(g):
        for k,o,n,ok,key in pieces(g):
            ref=patch(k,o,n,y,z)
            go=jnp.logical_and(ok,z>=k)
            tr.recv(jnp.logical_and(go,x!=0),ref,tr.slots("LB"+key,1))
            sem=tr.slots("LC"+key,3)
            for i in (1,2,3):
                a,b=at(y,core,x,up(z,i))
                lead_sent[k].append(tr.send(go,ref,ref,sem+i-1,a,b))
    def lead_d(g):
        for k,o,n,ok,key in pieces(g):
            sem=tr.slots("LC"+key,3)
            for i in (1,2,3):
                U=up(z,4-i)
                tr.recv(jnp.logical_and(ok,U>=k),patch(k,o,n,y,U),sem+i-1)
            ref=window(k,o,n,y)
            sem=tr.slots("LD"+key,3); cs=tr.slots("LE"+key,4)
            for i in (1,2,3):
                a,b=at(up(y,i),core,x,z)
                lead_sent[k].append(tr.send(ok,ref,ref,sem+i-1,a,b))
            a,b=at(y,1-core,x,z)
            lead_sent[k].append(tr.send(ok,ref,ref,cs,a,b))
    def lead_e(g):
        for k,o,n,ok,key in pieces(g):
            sem=tr.slots("LD"+key,3); cs=tr.slots("LE"+key,4)
            for i in (1,2,3):
                ref=window(k,o,n,up(y,4-i))
                tr.recv(ok,ref,sem+i-1)
                a,b=at(y,1-core,x,z)
                lead_sent[k].append(tr.send(ok,ref,ref,cs+i,a,b))
    def lead_wait(g):
        for k,o,n,ok,key in pieces(g):
            cs=tr.slots("LE"+key,4)
            for i in range(4):
                tr.recv(jnp.logical_not(ok),window(k,o,n,up(y,4-i)),cs+i)
    def lead_free(K):
        for n in lead_sent[K]:
            tr.settle(n,None)
            settled.add(n)
    settled=set()

    B=tr.slots("B",8); BD=tr.slots("BD",8)
    own=[]
    def b_first(q):
        own.append(tr.local(low,strip.at[q],col_out.at[rs,q]))
        for i in (1,3):
            a,b=at(up(y,i),core,x,z)
            tr.send(low,strip.at[q],col_out.at[rs,q],B+jnp.minimum(y,1)*4+q,a,b)
    def b_forward(q):
        f=jnp.clip(3-y,0,1)
        tr.recv(y>=2,col_out.at[2*f+core,q],B+f*4+q)
        a,b=at(jnp.clip(5-y,0,3),core,x,z)
        tr.send(y>=2,col_out.at[2*f+core,q],col_out.at[2*f+core,q],B+f*4+q,a,b)
    def b_last(q):
        o=jnp.where(y>=2,y-2,1-y)
        tr.recv(None,col_out.at[2*o+core,q],B+o*4+q)
        own[q]()
    def b_share(q):
        a,b=at(y,1-core,x,z)
        for j in (0,1):
            tr.send(None,col_out.at[2*j+core,q],col_out.at[2*j+core,q],BD+j*4+q,a,b)
    def b_done(q):
        for j in (0,1):
            tr.recv(None,col_out.at[2*j+1-core,q],BD+j*4+q)

    CS=tr.slots("CS",4); CST=tr.slots("CST",4); CSF=tr.slots("CSF",4)
    crow={}
    def c_scatter(q):
        for xx in (1,3):
            a,b=at(y,core,xx,z)
            tr.send(x0,panel.at[512*xx+128*q:512*xx+128*q+128,:],rowpart(xx,z,128*q,128),CS+q,a,b)
            if xx==(1 if q<2 else 3):
                tr.send(x0,panel.at[1024+128*q:1152+128*q,:],stage.at[128*(q%2):128*(q%2)+128,:],CST+q,a,b)
        crow[q]=tr.local(x0,panel.at[128*q:128*q+128,:],rowpart(0,z,128*q,128))
    def c_forward(q):
        via=x==(1 if q<2 else 3)
        ref=stage.at[128*(q%2):128*(q%2)+128,:]
        tr.recv(via,ref,CST+q)
        a,b=at(y,core,2,z)
        tr.send(via,ref,rowpart(2,z,128*q,128),CSF+q,a,b)
    def c_have(q):
        tr.recv(x13,rowpart(x,z,128*q,128),CS+q)
        tr.recv(x2,rowpart(x,z,128*q,128),CSF+q)
        crow[q]()

    AG=tr.slots("AG",60)
    orders=[[(q+i)%4 for i in range(4)] for q in range(4)]
    def ag_send(i,qs=range(4)):
        for q in qs:
            dims=orders[q]
            xx,zz=flip(dims[i],x,z)
            a,b=at(y,core,xx,zz)
            for m,(bx,bz) in enumerate(orbit(dims[:i],x,z)):
                ref=rowpart(bx,bz,128*q,128)
                tr.send(None,ref,ref,AG+q*15+(1<<i)-1+m,a,b)
    def ag_recv(i):
        for q in range(4):
            dims=orders[q]
            xx,zz=flip(dims[i],x,z)
            for m,(bx,bz) in enumerate(orbit(dims[:i],xx,zz)):
                tr.recv(None,rowpart(bx,bz,128*q,128),AG+q*15+(1<<i)-1+m)
    def more(n):
        for e in EVENTS.get(n,[]): eval_event(e)
    table={"lead_a":lead_a,"lead_b":lead_b,"lead_c":lead_c,"lead_d":lead_d,"lead_e":lead_e,"lead_wait":lead_wait,"lead_free":lead_free,
        "b_first":b_first,"b_forward":b_forward,"b_last":b_last,"b_share":b_share,"b_done":b_done,
        "c_scatter":c_scatter,"c_forward":c_forward,"c_have":c_have,"ag_send":ag_send,"ag_recv":ag_recv}
    def eval_event(e):
        table[e[0]](*e[1:])
    chol_events(u,w,us,ws,more)
    solve_columns(col_out,u,w,uh,ul,wh,wl,yh,yl)
    blk=u[pl.ds(pl.multiple_of(jnp.minimum(c,3)*T,T),T),pl.ds(pl.multiple_of(jnp.minimum(r,3)*T,T),T)]
    l_out[...]=blk.T
    more("end")
    tr.drain(settled)


EVENTS={
    "start":[("lead_a",0),("lead_a",1),("c_scatter",1),("lead_b",0),("c_scatter",3),("lead_c",0),("lead_b",1),("c_scatter",0),
        ("lead_d",0),("lead_c",1),("c_scatter",2),("c_forward",1),("lead_e",0),("lead_d",1),("c_forward",3),("c_have",1),("ag_send",0,(1,)),("lead_wait",0)],
    "0a":[("lead_free",0),("c_forward",0),("c_have",3),("ag_send",0,(3,)),("lead_e",1),("c_forward",2),("c_have",0),("c_have",2),("ag_send",0,(0,2))],
    0:[("b_first",0),("b_first",1),("b_first",2),("b_first",3)],
    "1a":[("lead_wait",1),("ag_recv",0),("ag_send",1)],
    1:[("lead_free",1),("lead_free",2),("lead_free",3)],
    "2a":[("ag_recv",1),("ag_send",2),("b_forward",0)],
    2:[("b_forward",1)],
    3:[("b_forward",2),("b_forward",3)],
    "4a":[("ag_recv",2),("ag_send",3)],
    5:[("b_last",q) for q in range(4)]+[("b_share",q) for q in range(4)],
    7:[("b_done",q) for q in range(4)],
    "end":[("ag_recv",3)],
}


def chol_events(u,w,us,ws,more):
    H=128
    more("start")
    for K in range(4):
        ko=T*K
        if K:
            u[ko:ko+T,ko:]=u[ko:ko+T,ko:]-dotx(u[:ko,ko:ko+T],u[:ko,ko:],TN)
            u[ko:ko+T,:ko]=jnp.zeros((T,ko),F32)
        Ws=[]
        for h in range(2):
            o=ko+H*h
            block128(u[o:o+H,o:o+H],us,ws)
            more("%da"%(2*K+h))
            ii,jj=iotas(H,H)
            W=jnp.where(jj<=ii,ws[...],0.0)
            n=1024-ko
            ri,ci=iotas(H,n)
            U=jnp.where(ci>=ri+H*h,dotx(W,u[o:o+H,ko:]),0.0)
            u[o:o+H,ko:]=U
            if h==0:
                u[o+H:o+T,ko:]=u[o+H:o+T,ko:]-dotx(U[:,H:T],U,TN)
                w[K,:H,:H]=W
                w[K,:H,H:]=jnp.zeros((H,H),F32)
                L21=dotx(U[:,H:T],W,TN)
            else:
                w[K,H:,H:]=W
                w[K,H:,:H]=-dotx(W,L21)
            more(2*K+h)


def solve_columns(cols,u,w,uh,ul,wh,wl,yh,yl):
    for k in range(4):
        ks=slice(k*T,(k+1)*T)
        uh[ks,:],ul[ks,:]=split(u[ks,:])
        wh[k],wl[k]=split(w[k])
        acc=jnp.concatenate([cols[k,q] for q in range(4)],axis=1)
        if k:
            acc=acc-dot3((uh[:k*T,ks],ul[:k*T,ks]),(yh[:k*T,:],yl[:k*T,:]),TN)
        yh[ks,:],yl[ks,:]=split(dot3((wh[k],wl[k]),split(acc)))


def gather_factor(panel,strip):
    any_=pl.BlockSpec(memory_space=pl.ANY); vm=pl.BlockSpec(memory_space=pltpu.VMEM)
    full=jax.ShapeDtypeStruct((1024,1024),BF); diag=jax.ShapeDtypeStruct((4,256,256),BF)
    return pl.pallas_call(gather_factor_kernel,
        out_shape=[jax.ShapeDtypeStruct((4,2048,256),F32),jax.ShapeDtypeStruct((256,256),F32),full,full,diag,diag,full,full],
        in_specs=[any_,any_],out_specs=[any_]+[vm]*7,
        scratch_shapes=[pltpu.VMEM((1024,1024),F32),pltpu.VMEM((4,256,256),F32),pltpu.VMEM((4,4,256,256),F32)]+[pltpu.VMEM((128,128),F32)]*2
            +[pltpu.VMEM((256,256),F32),pltpu.SemaphoreType.DMA((220,)),pltpu.SemaphoreType.DMA((150,))],
        compiler_params=pltpu.CompilerParams(vmem_limit_bytes=48<<20,collective_id=0,has_side_effects=True),name="gather_factor")(panel,strip)


def per_device(kernel):
    r=lax.axis_index("row"); c=lax.axis_index("col")
    panel=kernel[:,:,0,:].reshape(2048,256)
    strip=kernel[0].transpose(1,0,2)
    rows,*rest=gather_factor(panel,strip)
    pos=jnp.stack([r,c]).astype(jnp.int32)
    return finish(pos,kernel,rows,*rest)


def solution(mesh):
    spec=P(None,"row",None,"col")
    return jax.shard_map(per_device,mesh=mesh,in_specs=(spec,),out_specs=spec,check_vma=False)
```

time: 163 us -> 152 us (0.933)
  Pallas kernels: 160 us -> 143 us
  local copies, waits for them, and re-layouts: 3 us -> 7.47 us
    pallas_call x1, Pallas kernels: 118 us -> 102 us  [gather_factor(): pl.pallas_call(gather_factor_kernel, out_shape=[jax.ShapeDtypeStruct((4,...]
    unnamed x4 -> x10, local copies, waits for them, and re-layouts: 1.31 us -> 5.27 us
where the time goes in v3:
time: 152 us; the launch traced here: 151 us
  Pallas kernels  143 us (94%)
  local copies, waits for them, and re-layouts  7.47 us (5%)
    pallas_call x1, Pallas kernels, gather_factor(): pl.pallas_call(gather_factor_kernel, out_shape=[jax.ShapeDtypeStruct((4,...  102 us
    pallas_call x1, Pallas kernels, finish(): pl.pallas_call(finish_kernel, grid=(8,), in_specs=[pl.BlockSpec(memory_sp...  40.5 us
    unnamed x10, local copies, waits for them, and re-layouts  5.27 us

profile of v3, /device:TPU:18, one launch (start us, length us, event | category | flops | bytes accessed | tf_op | source)
XLA Modules:
  0.0 151.0 jit_solution(973313613502324425)
XLA Ops:
  0.0 0.0 slice-start
  0.0 0.6 pad_add_fusion.pos
  0.6 0.6 slice-done
  1.2 0.2 copy.8
  1.4 0.0 slice-start.1
  1.4 1.6 %slice-done.1 = f32[8,256,1,256]{3,2,1,0:T(1,128)S(1)} async-done(((f32[8,256,4,256]{3,2,1,0:T(4,128)}), f32[8,256,1,256]{3,2,1,0:T(1,128)S(1)}, s32[]{:S(2)}) %slice-start.1) | async-done | bytes 2097176 | tf_op jit(solution)/shard_map/slice | solution.py:402
  3.0 1.5 copy.5
  4.5 102.3 %gather_factor.1 = (f32[4,2048,256]{2,1,0:T(8,128)}, f32[256,256]{1,0:T(8,128)S(1)}, bf16[1024,1024]{1,0:T(8,128)(2,1)S(1)}, bf16[1024,1024]{1,0:T(8,128)(2,1)},...) custom-call(f32[2048,256]{1,0:T(8,128)} %bitcast.9, ...), custom_call_target="tpu_custom_call" | custom-call | tf_op jit(solution)/shard_map/gather_factor/pallas_call | solution.py:392
  106.8 0.0 copy-start
  106.8 1.3 copy-done
  108.1 0.0 copy-start.1
  108.1 0.8 copy-done.1
  108.9 0.0 copy-start.2
  109.0 0.8 copy-done.2
  109.7 0.0 copy-start.3
  109.7 0.7 copy-done.3
  110.5 40.5 %finish.1 = f32[8,256,4,256]{3,2,1,0:T(4,128)} custom-call(s32[2]{0:T(128)} %pad_add_fusion.pos, f32[8,256,4,256]{3,2,1,0:T(4,128)} %ker.1, f32[4,2048,256]{2,1,0:T(8,128)} %get-tuple-element.13.rows, f32[256,256]{1,0:T(8,128)} %copy-done.3, bf16[1024,1024]{1,0:T(8,128)(2,1)} %copy-done, bf16[1024,1024]{1,0:T(8,128)(2,1)} %get-tuple-element.16.ul, ...), custom_call_target="tpu_custom_call" | custom-call | tf_op jit(solution)/shard_map/finish/pallas_call | solution.py:50
Async XLA Ops:
  0.0 1.2 slice-start
  1.4 1.6 %slice-start.1 = ((f32[8,256,4,256]{3,2,1,0:T(4,128)}), f32[8,256,1,256]{3,2,1,0:T(1,128)S(1)}, s32[]{:S(2)}) async-start(f32[8,256,4,256]{3,2,1,0:T(4,128)} %ker.1), calls=%async_computation.1 | async-start | bytes 4194304 | tf_op jit(solution)/shard_map/slice | solution.py:402
  106.8 1.3 copy-start
  108.1 0.8 copy-start.1
  108.9 0.8 copy-start.2
  109.7 0.7 copy-start.3

commit v4 on v3

--- a/solution.py
+++ b/solution.py
@@ -19,40 +19,41 @@
 
 def finish_kernel(pos,ker,rows,l_blk,uh,ul,wh,wl,yh,yl,out,xh,xl,xp):
     t=pl.program_id(0); r=pos[0]; c=pos[1]
-    lead=jnp.logical_and(t==0,r<4)
-    @pl.when(lead)
+    n=ker.shape[0]
+    for k in range(4):
+        ks=slice(k*T,(k+1)*T)
+        acc=rows[k]
+        if k:
+            acc=acc-dot3((xh[:,:k*T],xl[:,:k*T]),(uh[:k*T,ks],ul[:k*T,ks]))
+        x=dot3(split(acc),(wh[k],wl[k]),NT)
+        xh[:,ks],xl[:,ks]=split(x)
+        xp[:,ks]=x
+    for uu in range(4):
+        us=slice(uu*T,(uu+1)*T)
+        s=dot3((xh[...],xl[...]),(yh[:,us],yl[:,us]))
+        for i in range(n):
+            out[i,:,uu,:]=ker[i,:,uu,:]-s[i*T:(i+1)*T]
+    @pl.when(c<4)
     def _():
-        out[...]=jnp.zeros_like(out)
+        for i in range(n):
+            out[i,:,0,:]=xp[i*T:(i+1)*T,pl.ds(pl.multiple_of(jnp.minimum(c,3)*T,T),T)]
+    @pl.when(jnp.logical_and(t==0,r<4))
+    def _():
+        out[0]=jnp.zeros_like(out[0])
         @pl.when(c<4)
         def _():
             out[0,:,0,:]=l_blk[...]
-    @pl.when(jnp.logical_not(lead))
-    def _():
-        for k in range(4):
-            ks=slice(k*T,(k+1)*T)
-            acc=rows[k]
-            if k:
-                acc=acc-dot3((xh[:,:k*T],xl[:,:k*T]),(uh[:k*T,ks],ul[:k*T,ks]))
-            x=dot3(split(acc),(wh[k],wl[k]),NT)
-            xh[:,ks],xl[:,ks]=split(x)
-            xp[:,ks]=x
-        for uu in range(4):
-            us=slice(uu*T,(uu+1)*T)
-            s=dot3((xh[...],xl[...]),(yh[:,us],yl[:,us]))
-            out[0,:,uu,:]=ker[0,:,uu,:]-s
-        @pl.when(c<4)
-        def _():
-            out[0,:,0,:]=xp[:,pl.ds(pl.multiple_of(jnp.minimum(c,3)*T,T),T)]
 
 
 def finish(pos,kernel,rows,*rest):
+    n=2
     full=lambda a: pl.BlockSpec(a.shape,lambda t:(0,)*a.ndim,pipeline_mode=pl.Buffered(1))
-    return pl.pallas_call(finish_kernel,grid=(8,),
-        in_specs=[pl.BlockSpec(memory_space=pltpu.SMEM),pl.BlockSpec((1,256,4,256),lambda t:(t,0,0,0)),
-                  pl.BlockSpec((4,256,256),lambda t:(0,t,0))]+[full(a) for a in rest],
-        out_specs=pl.BlockSpec((1,256,4,256),lambda t:(t,0,0,0)),
+    return pl.pallas_call(finish_kernel,grid=(8//n,),
+        in_specs=[pl.BlockSpec(memory_space=pltpu.SMEM),pl.BlockSpec((n,256,4,256),lambda t:(t,0,0,0)),
+                  pl.BlockSpec((4,n*256,256),lambda t:(0,t,0))]+[full(a) for a in rest],
+        out_specs=pl.BlockSpec((n,256,4,256),lambda t:(t,0,0,0)),
         out_shape=jax.ShapeDtypeStruct((8,256,4,256),F32),
-        scratch_shapes=[pltpu.VMEM((256,1024),BF)]*2+[pltpu.VMEM((256,1024),F32)],
+        scratch_shapes=[pltpu.VMEM((n*256,1024),BF)]*2+[pltpu.VMEM((n*256,1024),F32)],
         compiler_params=pltpu.CompilerParams(vmem_limit_bytes=56<<20),name="finish")(pos,kernel,rows,*rest)
 
 
@@ -330,15 +331,14 @@
 
 EVENTS={
     "start":[("lead_a",0),("lead_a",1),("c_scatter",1),("lead_b",0),("c_scatter",3),("lead_c",0),("lead_b",1),("c_scatter",0),
-        ("lead_d",0),("lead_c",1),("c_scatter",2),("c_forward",1),("lead_e",0),("lead_d",1),("c_forward",3),("c_have",1),("ag_send",0,(1,)),("lead_wait",0)],
-    "0a":[("lead_free",0),("c_forward",0),("c_have",3),("ag_send",0,(3,)),("lead_e",1),("c_forward",2),("c_have",0),("c_have",2),("ag_send",0,(0,2))],
+        ("lead_d",0),("lead_c",1),("c_scatter",2),("c_forward",1),("lead_e",0),("c_forward",3),("c_have",1),("ag_send",0,(1,)),("c_have",3),("ag_send",0,(3,)),("lead_wait",0)],
+    "0a":[("lead_free",0),("lead_d",1),("c_forward",0),("c_forward",2),("c_have",0),("c_have",2),("ag_send",0,(0,2)),("lead_e",1)],
     0:[("b_first",0),("b_first",1),("b_first",2),("b_first",3)],
     "1a":[("lead_wait",1),("ag_recv",0),("ag_send",1)],
-    1:[("lead_free",1),("lead_free",2),("lead_free",3)],
-    "2a":[("ag_recv",1),("ag_send",2),("b_forward",0)],
+    1:[("lead_free",1),("lead_free",2),("lead_free",3),("ag_recv",1),("ag_send",2)],
+    "2a":[("b_forward",0)],
     2:[("b_forward",1)],
-    3:[("b_forward",2),("b_forward",3)],
-    "4a":[("ag_recv",2),("ag_send",3)],
+    3:[("ag_recv",2),("ag_send",3),("b_forward",2),("b_forward",3)],
     5:[("b_last",q) for q in range(4)]+[("b_share",q) for q in range(4)],
     7:[("b_done",q) for q in range(4)],
     "end":[("ag_recv",3)],

time: 152 us -> 151 us (level)
  Pallas kernels: 143 us -> 141 us
    pallas_call x1, Pallas kernels: 40.5 us -> 38.1 us  [finish(): pl.pallas_call(finish_kernel, grid=(8 // n,), in_specs=[pl.BlockSpec(memo...]
where the time goes in v4:
time: 151 us; the launch traced here: 149 us
  Pallas kernels  141 us (93%)
  local copies, waits for them, and re-layouts  7.47 us (5%)
    pallas_call x1, Pallas kernels, gather_factor(): pl.pallas_call(gather_factor_kernel, out_shape=[jax.ShapeDtypeStruct((4,...  103 us
    pallas_call x1, Pallas kernels, finish(): pl.pallas_call(finish_kernel, grid=(8 // n,), in_specs=[pl.BlockSpec(memo...  38.1 us
    unnamed x10, local copies, waits for them, and re-layouts  5.27 us

profile of v4, /device:TPU:18, one launch (start us, length us, event | category | flops | bytes accessed | tf_op | source)
XLA Modules:
  0.0 149.2 jit_solution(15760900686602180450)
XLA Ops:
  0.0 0.0 slice-start
  0.0 0.6 pad_add_fusion.pos
  0.6 0.6 slice-done
  1.2 0.2 copy.8
  1.4 0.0 slice-start.1
  1.4 1.6 %slice-done.1 = f32[8,256,1,256]{3,2,1,0:T(1,128)S(1)} async-done(((f32[8,256,4,256]{3,2,1,0:T(4,128)}), f32[8,256,1,256]{3,2,1,0:T(1,128)S(1)}, s32[]{:S(2)}) %slice-start.1) | async-done | bytes 2097176 | tf_op jit(solution)/shard_map/slice | solution.py:402
  3.0 1.5 copy.5
  4.5 102.9 %gather_factor.1 = (f32[4,2048,256]{2,1,0:T(8,128)}, f32[256,256]{1,0:T(8,128)S(1)}, bf16[1024,1024]{1,0:T(8,128)(2,1)S(1)}, bf16[1024,1024]{1,0:T(8,128)(2,1)},...) custom-call(f32[2048,256]{1,0:T(8,128)} %bitcast.9, ...), custom_call_target="tpu_custom_call" | custom-call | tf_op jit(solution)/shard_map/gather_factor/pallas_call | solution.py:392
  107.4 0.0 copy-start
  107.4 1.3 copy-done
  108.7 0.0 copy-start.1
  108.7 0.8 copy-done.1
  109.6 0.0 copy-start.2
  109.6 0.8 copy-done.2
  110.3 0.0 copy-start.3
  110.3 0.7 copy-done.3
  111.1 38.1 %finish.1 = f32[8,256,4,256]{3,2,1,0:T(4,128)} custom-call(s32[2]{0:T(128)} %pad_add_fusion.pos, f32[8,256,4,256]{3,2,1,0:T(4,128)} %ker.1, f32[4,2048,256]{2,1,0:T(8,128)} %get-tuple-element.13.rows, f32[256,256]{1,0:T(8,128)} %copy-done.3, bf16[1024,1024]{1,0:T(8,128)(2,1)} %copy-done, bf16[1024,1024]{1,0:T(8,128)(2,1)} %get-tuple-element.16.ul, ...), custom_call_target="tpu_custom_call" | custom-call | tf_op jit(solution)/shard_map/finish/pallas_call | solution.py:51
Async XLA Ops:
  0.0 1.2 slice-start
  1.4 1.6 %slice-start.1 = ((f32[8,256,4,256]{3,2,1,0:T(4,128)}), f32[8,256,1,256]{3,2,1,0:T(1,128)S(1)}, s32[]{:S(2)}) async-start(f32[8,256,4,256]{3,2,1,0:T(4,128)} %ker.1), calls=%async_computation.1 | async-start | bytes 4194304 | tf_op jit(solution)/shard_map/slice | solution.py:402
  107.4 1.3 copy-start
  108.7 0.8 copy-start.1
  109.6 0.8 copy-start.2
  110.3 0.7 copy-start.3
